TPU v7x, 128 devices: a whole 4x4x4 slice. The times are simulated.
128 devices in a mesh: band: 8 (over z, core), strip: 16 (over y, x).
Axes of the slice: x: 4, y: 4, z: 4, core: 2. Of those that a mesh axis runs over, the one named last changes fastest.
Arguments:
- first_scene: bfloat16 [4096, 8192], P('band', 'strip'), may hold values from -6 to 6
- second_scene: bfloat16 [4096, 8192], P('band', 'strip'), may hold values from -6 to 6
- owner_strip: int32 [8, 16, 16, 1], P('band', 'strip'), may hold values from 0 to 15; in each aligned block of 16 rows (0 to 15, 16 to 31, ..., all dimensions but the last counted through in order) at most 2 rows name the same one
- target_tile: int32 [8, 16, 16], P('band', 'strip'), may hold values from 0 to 15
- offsets: int32 [8, 16, 16, 2], P('band', 'strip'), may hold values from -32 to 32
- valid_mask: int32 [8, 16, 16], P('band', 'strip'), may hold values 0 or 1
Outputs:
- consistency: float32 [8, 16, 16, 4096], P('band', 'strip')
Inputs may be any that keep to these rules, and one draw needn't show every extreme that they name: `owner_strip`: among the 16 patches of one device at most 2 name the same owner strip, and in every draw some device has 2 patches naming one strip.
All inputs are finite; a program needn't handle non-finite values. No bound on the sum of `valid_mask` on one device may be relied on, other than what follows from the above.
Results may differ from a plain program's by a relative error of at most 0.0003.
Values may be sent and summed in bfloat16 or wider, within the bound.
No kernel may reach another device: no remote copies, remote signals or barrier semaphores. Data moves between devices by JAX's collectives and lax.ppermute only.
A program may use at most 128 MiB of HBM per device.

v0:
```python
import jax
import jax.numpy as jnp
from jax import lax
from jax.experimental import pallas as pl
from jax.experimental.pallas import tpu as pltpu
from jax.sharding import PartitionSpec as P

SIDE = 128
SHIFTS = 64
SEARCH = 192
HALO = 64
EPSILON = 1e-05
COLS = 22
BANDS = 3
ROWS = 16
SPAN = 80
BLOCKS = SIDE // ROWS
DEPTH = BLOCKS * SIDE + 256
PACKED = SEARCH + SEARCH // 2
EXTRA = 32
TALL = COLS * ROWS + EXTRA
DIMS = (((1,), (1,)), ((), ()))


def lane_iota(shape):
    return lax.broadcasted_iota(jnp.int32, shape, len(shape) - 1)


def cut_kernel(requests, scene_ref, out_ref, wide):
    for part in range(5):
        wide[part] = scene_ref[:, 128 * part : 128 * (part + 1)].astype(jnp.float32)
    wide[5] = jnp.zeros((640, 128), jnp.float32)
    lanes = lane_iota((SEARCH, 128))
    lower = lane_iota((SEARCH // 2, 128)) < 64

    def one(slot, carry):
        top = requests[slot // 2, slot % 2, 0]
        left = requests[slot // 2, slot % 2, 1]
        base = left // 128
        rest = left % 128
        turn = (128 - rest) % 128
        turned = [
            pltpu.roll(wide[base + part, pl.ds(top, SEARCH), :], turn, 1) for part in range(3)
        ]
        inside = lanes < 128 - rest
        near = jnp.where(inside, turned[0], turned[1])
        far = jnp.where(inside, turned[1], turned[2])
        out_ref[slot, :SEARCH, :] = near.astype(jnp.bfloat16)
        half = SEARCH // 2
        mixed = jnp.where(lower, far[:half], pltpu.roll(far[half:], 64, 1))
        out_ref[slot, SEARCH:, :] = mixed.astype(jnp.bfloat16)
        return carry

    lax.fori_loop(0, out_ref.shape[0], one, 0)


def cut_windows(scene, requests):
    slots = 2 * requests.shape[0]
    return pl.pallas_call(
        cut_kernel,
        out_shape=jax.ShapeDtypeStruct((slots, PACKED, 128), jnp.bfloat16),
        in_specs=[
            pl.BlockSpec(memory_space=pltpu.SMEM),
            pl.BlockSpec(memory_space=pltpu.VMEM),
        ],
        out_specs=pl.BlockSpec(memory_space=pltpu.VMEM),
        scratch_shapes=[pltpu.VMEM((6, 640, 128), jnp.float32)],
        compiler_params=pltpu.CompilerParams(vmem_limit_bytes=32 * 1024 * 1024),
        name="cut_windows",
    )(requests, scene)


def normalize(patch):
    centered = patch - jnp.mean(patch)
    return centered * lax.rsqrt(jnp.mean(centered * centered) + EPSILON)


def exchange(size):
    rows = lax.broadcasted_iota(jnp.int32, (size, size), 0)
    return (rows + lane_iota((size, size)) == size - 1).astype(jnp.bfloat16)


def halves(values):
    high = values.astype(jnp.bfloat16)
    low = (values - high.astype(jnp.float32)).astype(jnp.bfloat16)
    return high, low


def spread_template(values, left, row_at, lane_at, reverse):
    lanes = lane_iota((ROWS, 128)).astype(jnp.int16)
    groups = (lane_iota((ROWS, 128)) // 32).astype(jnp.int16)
    within = (lane_iota((ROWS, 128)) % 32).astype(jnp.int16)
    zero = jnp.zeros((ROWS, 128), jnp.bfloat16)
    blocks = [values[ROWS * q : ROWS * (q + 1)] for q in range(BLOCKS)]
    ends = []
    for group in range(2):
        end = zero
        for part in range(4):
            turned = pltpu.roll(blocks[4 * group + part], 32 * part, 1)
            end = jnp.where(groups == (part + 3) % 4, turned, end)
        ends.append(end)
    for a in range(COLS):
        shift = COLS - 1 - a if reverse else a
        rows = pl.ds(row_at + ROWS * a, ROWS)
        for q in range(BLOCKS):
            moved = pltpu.roll(blocks[q], shift, 1)
            moved = jnp.where(lanes >= shift, moved, zero)
            left[rows, pl.ds(lane_at + 128 * q, 128)] = moved
        for group in range(2):
            moved = pltpu.roll(ends[group], shift, 1)
            moved = jnp.where(within < shift, moved, zero)
            left[rows, pl.ds(lane_at + 128 * (BLOCKS + group), 128)] = moved


def spread_window(near, far, right, lane_at, offsets):
    lanes = lane_iota((SEARCH, 128)).astype(jnp.int16)
    for b, offset in enumerate(offsets):
        back = (128 - offset) % 128
        main = near
        if offset:
            main = jnp.where(
                lanes < 128 - offset, pltpu.roll(near, back, 1), pltpu.roll(far, back, 1)
            )
        rows = pl.ds(SPAN * b, SPAN)
        for q in range(BLOCKS):
            right[rows, pl.ds(lane_at + 128 * q, 128)] = main[ROWS * q : ROWS * q + SPAN]
        turned = [pltpu.roll(far, (back + 32 * part) % 128, 1) for part in range(4)]
        few = (lane_iota((SPAN, 128)) // 32).astype(jnp.int16)
        for group in range(2):
            tail = turned[0][ROWS * 4 * group : ROWS * 4 * group + SPAN]
            for part in range(1, 4):
                q = 4 * group + part
                tail = jnp.where(few == part, turned[part][ROWS * q : ROWS * q + SPAN], tail)
            right[rows, pl.ds(lane_at + 128 * (BLOCKS + group), 128)] = tail


def fold_diagonals(product):
    cube = product.reshape(COLS, ROWS, 256)
    level = lax.broadcasted_iota(jnp.int32, (COLS * 8, 256), 0) % 8
    part = cube[:, :8].reshape(COLS * 8, 256) + pltpu.roll(
        cube[:, 8:].reshape(COLS * 8, 256), 248, 1
    )
    for bit in (4, 2, 1):
        part = jnp.where(level & bit != 0, pltpu.roll(part, 256 - bit, 1), part)
    return jnp.sum(part.reshape(COLS, 8, 256), axis=1)


def search_block(windows_ref, slot):
    near = windows_ref[slot, :SEARCH, :]
    packed = windows_ref[slot, SEARCH:, :]
    return near, jnp.concatenate([packed, pltpu.roll(packed, 64, 1)], axis=0)


def flipped_centre(near, far):
    flip = exchange(128)
    low, high = [
        jnp.dot(flip, part[32:160], preferred_element_type=jnp.float32) for part in (near, far)
    ]
    lanes = lane_iota((128, 128))
    return jnp.where(lanes < 96, pltpu.roll(low, 96, 1), pltpu.roll(high, 96, 1))


def flipped_around(beside_ref, row, col):
    return jnp.dot(
        exchange(SEARCH),
        beside_ref[pl.ds(row + 32, SEARCH), pl.ds(col, 256)],
        preferred_element_type=jnp.float32,
    ).astype(jnp.bfloat16)


def place_of(patch):
    return pl.multiple_of(patch // 4 * 128, 128), pl.multiple_of(patch % 4 * 128, 128)


def careful_kernel(slots, first_ref, beside_ref, windows_ref, out_ref, left, right):
    right[SPAN * BANDS :, :] = jnp.zeros((256 - SPAN * BANDS, 2 * DEPTH), jnp.bfloat16)
    count = COLS * ROWS

    def one(patch, carry):
        row, col = place_of(patch)
        near, far = search_block(windows_ref, slots[patch])
        template = normalize(first_ref[pl.ds(row, 128), pl.ds(col, 128)].astype(jnp.float32))
        centre = flipped_centre(near, far)
        around = flipped_around(beside_ref, row, col)
        inner = first_ref[pl.ds(row, 128), pl.ds(col, 128)].astype(jnp.float32)
        sides = ((template, jnp.mean(centre), False), (normalize(centre), jnp.mean(inner), True))
        rest = jnp.float32(0.0)
        for place, (values, level, reverse) in enumerate(sides):
            high, low = halves(values)
            for half, piece in enumerate((high, low)):
                spread_template(piece, left, count * half, DEPTH * place, reverse)
            rest += level * (
                jnp.sum(high.astype(jnp.float32)) + jnp.sum(low.astype(jnp.float32))
            )
        spread_window(near, far, right, 0, (0, 22, 44))
        spread_window(around[:, :128], around[:, 128:], right, DEPTH, (75, 53, 31))
        both = lax.dot_general(left[...], right[...], DIMS, preferred_element_type=jnp.float32)
        out_ref[patch] = fold_diagonals(both[:count] + both[count:]) - rest
        return carry

    lax.fori_loop(0, 16, one, 0)


def careful_surfaces(slots, first, beside, windows):
    return pl.pallas_call(
        careful_kernel,
        out_shape=jax.ShapeDtypeStruct((16, COLS, 256), jnp.float32),
        in_specs=[pl.BlockSpec(memory_space=pltpu.SMEM)]
        + [pl.BlockSpec(memory_space=pltpu.VMEM)] * 3,
        out_specs=pl.BlockSpec(memory_space=pltpu.VMEM),
        scratch_shapes=[
            pltpu.VMEM((2 * COLS * ROWS, 2 * DEPTH), jnp.bfloat16),
            pltpu.VMEM((256, 2 * DEPTH), jnp.bfloat16),
        ],
        compiler_params=pltpu.CompilerParams(vmem_limit_bytes=40 * 1024 * 1024),
        name="careful_surfaces",
    )(slots, first, beside, windows)


def ones_rows(left, reverse):
    index = lax.broadcasted_iota(jnp.int32, (EXTRA, 128), 0)
    lanes = lane_iota((EXTRA, 128))
    shift = COLS - 1 - index if reverse else index
    main = jnp.where((index < COLS) & (lanes >= shift), 1.0, 0.0).astype(jnp.bfloat16)
    tail = jnp.where((index < COLS) & (lanes % 32 < shift), 1.0, 0.0).astype(jnp.bfloat16)
    for q in range(BLOCKS):
        left[COLS * ROWS :, 128 * q : 128 * (q + 1)] = main
    for group in range(2):
        at = 128 * (BLOCKS + group)
        left[COLS * ROWS :, at : at + 128] = tail


def level_of(values):
    mean = jnp.mean(values)
    centered = values - mean
    spread = jnp.mean(centered * centered)
    large = jnp.where(mean * mean > 4.0 * spread, 1.0, 0.0)
    return mean, lax.rsqrt(jnp.full((1, 256), spread + EPSILON)), large


def prepare_kernel(first_ref, beside_ref, left_out, right_out, level_out):
    row, col = place_of(pl.program_id(0))
    left, right = left_out.at[0], right_out.at[0]
    tile = first_ref[pl.ds(row, 128), pl.ds(col, 128)]
    mean, scale, large = level_of(tile.astype(jnp.float32))
    level_out[0, 0:1, :] = scale * mean
    level_out[0, 1:2, :] = scale
    level_out[0, 2:3, :] = jnp.full((1, 256), large)
    level_out[0, 3:8, :] = jnp.zeros((5, 256), jnp.float32)
    spread_template(tile, left, 0, 0, False)
    ones_rows(left, False)
    around = flipped_around(beside_ref, row, col)
    spread_window(around[:, :128], around[:, 128:], right, 0, (75, 53, 31))
    right[SPAN * BANDS :, :] = jnp.zeros((256 - SPAN * BANDS, DEPTH), jnp.bfloat16)


def prepared(first, beside):
    whole = pl.BlockSpec(memory_space=pltpu.VMEM)
    shapes = ((TALL, DEPTH, jnp.bfloat16), (256, DEPTH, jnp.bfloat16), (8, 256, jnp.float32))
    return pl.pallas_call(
        prepare_kernel,
        grid=(16,),
        out_shape=[pltpu.HBM((16, m, n), kind) for m, n, kind in shapes],
        in_specs=[whole, whole],
        out_specs=[pl.BlockSpec((1, m, n), lambda k: (k, 0, 0)) for m, n, _ in shapes],
        compiler_params=pltpu.CompilerParams(vmem_limit_bytes=24 * 1024 * 1024),
        cost_estimate=pl.CostEstimate(
            flops=20_000_000_000, bytes_accessed=30_000_000, transcendentals=0
        ),
        name="prepare",
    )(first, beside)


def surface_kernel(
    slots, windows_ref, left_ref, right_ref, level_ref, out_ref, large_ref, *scratch
):
    step = pl.program_id(0)
    count = COLS * ROWS

    @pl.when(step == 0)
    def _():
        large_ref[0] = 0
        for left, right, side in (scratch[:3], scratch[3:]):
            right[SPAN * BANDS :, :] = jnp.zeros((256 - SPAN * BANDS, DEPTH), jnp.bfloat16)
            ones_rows(left, True)

    def both(building, using):
        left, right, side = using
        ahead = lax.dot_general(left_ref[0], right[...], DIMS, preferred_element_type=jnp.float32)
        behind = lax.dot_general(left[...], right_ref[0], DIMS, preferred_element_type=jnp.float32)
        raw = level_ref[0, 1:2, :] * ahead[:count] + side[1:2, :] * behind[:count]
        box = level_ref[0, 0:1, :] * ahead[count:] + side[0:1, :] * behind[count:]
        for shift in (1, 2, 4, 8):
            box = box + pltpu.roll(box, 256 - shift, 1)
        out_ref[0] = fold_diagonals(raw) - box[:COLS]

        left, right, side = building
        near, far = search_block(windows_ref, slots[jnp.minimum(step, 15)])
        centre = flipped_centre(near, far)
        spread_window(near, far, right, 0, (0, 22, 44))
        spread_template(centre.astype(jnp.bfloat16), left, 0, 0, True)
        mean, scale, large = level_of(centre)
        side[0:1, :] = scale * mean
        side[1:2, :] = scale
        large_ref[0] = jnp.maximum(
            large_ref[0], jnp.maximum(large, jnp.max(level_ref[0, 2:3, :])).astype(jnp.int32)
        )

    @pl.when(step % 2 == 0)
    def _():
        both(scratch[:3], scratch[3:])

    @pl.when(step % 2 == 1)
    def _():
        both(scratch[3:], scratch[:3])


def surfaces_of(slots, windows, left, right, level):
    def block(m, n):
        return pl.BlockSpec((1, m, n), lambda k: (jnp.maximum(k - 1, 0), 0, 0))

    return pl.pallas_call(
        surface_kernel,
        grid=(17,),
        out_shape=[
            jax.ShapeDtypeStruct((16, COLS, 256), jnp.float32),
            jax.ShapeDtypeStruct((1,), jnp.int32),
        ],
        in_specs=[
            pl.BlockSpec(memory_space=pltpu.SMEM),
            pl.BlockSpec(memory_space=pltpu.VMEM),
            block(TALL, DEPTH),
            block(256, DEPTH),
            block(8, 256),
        ],
        out_specs=[block(COLS, 256), pl.BlockSpec(memory_space=pltpu.SMEM)],
        scratch_shapes=[
            pltpu.VMEM((TALL, DEPTH), jnp.bfloat16),
            pltpu.VMEM((256, DEPTH), jnp.bfloat16),
            pltpu.VMEM((8, 256), jnp.float32),
        ]
        * 2,
        compiler_params=pltpu.CompilerParams(vmem_limit_bytes=24 * 1024 * 1024),
        cost_estimate=pl.CostEstimate(
            flops=20_000_000_000, bytes_accessed=30_000_000, transcendentals=0
        ),
        name="surfaces",
    )(slots, windows, left, right, level)


def combined(slots, first, beside, windows, ready):
    ready = [pltpu.with_memory_space_constraint(array, pltpu.HBM) for array in ready]
    folded, large = surfaces_of(slots, windows, *ready)
    return lax.cond(
        large[0] > 0,
        lambda: careful_surfaces(slots, first, beside, windows),
        lambda: folded,
    )


def finish(folded, mask):
    parts = folded[:, :, : SPAN * BANDS].reshape(16, COLS, BANDS, SPAN)[..., :SHIFTS]
    surface = parts.transpose(0, 3, 2, 1).reshape(16, SHIFTS, BANDS * COLS)[:, :, :SHIFTS]
    scale = mask.reshape(16, 1).astype(jnp.float32) / (2.0 * SIDE)
    return surface.reshape(16, SHIFTS * SHIFTS) * scale


def moved(values, axis, forward):
    count = lax.axis_size(axis)
    pairs = [(i, i + 1) if forward else (i + 1, i) for i in range(count - 1)]
    return lax.ppermute(values, axis, pairs)


def rows_around(first, second):
    from_above = moved(jnp.concatenate([first[-HALO:], second[-HALO:]], 1), "band", True)
    from_below = moved(jnp.concatenate([first[:HALO], second[:HALO]], 1), "band", False)
    return from_above, from_below


def with_margins(first, second, from_above, from_below):
    width = first.shape[1]
    first = jnp.concatenate([from_above[:, :width], first, from_below[:, :width]], 0)
    second = jnp.concatenate([from_above[:, width:], second, from_below[:, width:]], 0)
    from_left = moved(jnp.concatenate([first[:, -HALO:], second[:, -HALO:]], 1), "strip", True)
    from_right = moved(jnp.concatenate([first[:, :HALO], second[:, :HALO]], 1), "strip", False)
    first = jnp.concatenate([from_left[:, :HALO], first, from_right[:, :HALO]], 1)
    second = jnp.concatenate([from_left[:, HALO:], second, from_right[:, HALO:]], 1)
    return first, second


def to_owners(values):
    return lax.all_to_all(values, "strip", split_axis=0, concat_axis=0, tiled=True)


def on_device(first, second, owner_strip, target_tile, offsets, valid_mask):
    strips = lax.axis_size("strip")
    from_above, from_below = rows_around(first, second)
    order = jnp.arange(16, dtype=jnp.int32)
    owners = owner_strip.reshape(16)
    earlier = (owners[:, None] == owners[None, :]) & (order[None, :] < order[:, None])
    slot_of = owners * 2 + jnp.sum(earlier.astype(jnp.int32), axis=1)
    placing = (slot_of[:, None] == jnp.arange(2 * strips, dtype=jnp.int32)[None, :]).astype(jnp.int32)
    tiles = target_tile.reshape(16)
    shifts = offsets.reshape(16, 2)
    corner = jnp.stack(
        [tiles // 4 * SIDE + shifts[:, 0] + 32, tiles % 4 * SIDE + shifts[:, 1] + 32], axis=1
    )
    outgoing = jnp.sum(placing[:, :, None] * corner[:, None, :], axis=0).reshape(strips, 2, 2)
    outgoing, from_above, from_below = lax.optimization_barrier((outgoing, from_above, from_below))
    requests = to_owners(outgoing)
    beside, wide = with_margins(first, second, from_above, from_below)
    windows = cut_windows(wide, requests)
    windows = to_owners(windows.reshape(strips, 2 * PACKED, 128))
    windows = windows.reshape(2 * strips, PACKED, 128)
    folded = combined(slot_of, first, beside, windows, prepared(first, beside))
    return finish(folded, valid_mask).reshape(1, 1, 16, SHIFTS * SHIFTS)


def bench(slots, first, beside, windows, mask):
    return finish(combined(slots, first, beside, windows, prepared(first, beside)), mask)


def solution(mesh):
    return jax.shard_map(
        on_device,
        mesh=mesh,
        in_specs=(
            P("band", "strip"),
            P("band", "strip"),
            P("band", "strip", None, None),
            P("band", "strip", None),
            P("band", "strip", None, None),
            P("band", "strip", None),
        ),
        out_specs=P("band", "strip", None, None),
        check_vma=False,
    )
```

profile of v0, /device:TPU:1, one launch (start us, length us, event | category | flops | bytes accessed | tf_op | source)
XLA Modules:
  0.0 108.5 jit_solution(3754675673486486121)
XLA Ops:
  0.0 0.0 copy-start
  0.0 0.0 copy-start.2
  0.0 1.0 fusion.17
  1.1 4.9 %collective-permute-start = (bf16[64,1024]{1,0:T(8,128)(2,1)S(1)}, bf16[64,1024]{1,0:T(8,128)(2,1)S(1)}, u32[]{:S(2)}, u32[]{:S(2)}) collective-permute-start(bf16[64,1024]{1,0:T(8,128)(2,1)S(1)} %pad_maximum_fusion.6), channel_id=1, source_target_pairs={{0,16},{16,32},{32,48},{48,64},{64,80},{80,96},{96,112},{1,17},{17... | collective-permute-start | bytes 393224 | tf_op jit(solution)/shard_map/ppermute | solution.py:371
  6.0 1.9 %collective-permute-start.1 = (bf16[64,1024]{1,0:T(8,128)(2,1)S(1)}, bf16[64,1024]{1,0:T(8,128)(2,1)S(1)}, u32[]{:S(2)}, u32[]{:S(2)}) collective-permute-start(bf16[64,1024]{1,0:T(8,128)(2,1)S(1)} %pad_maximum_fusion.7), channel_id=1, source_target_pairs={{16,0},{32,16},{48,32},{64,48},{80,64},{96,80},{112,96},{17,1},{33... | collective-permute-start | bytes 393224 | tf_op jit(solution)/shard_map/ppermute | solution.py:371
  8.0 0.9 convert_reduce_fusion
  8.9 0.7 multiply_add_fusion.slots
  9.5 0.1 fusion.13
  9.6 0.8 add_add_fusion
  10.4 0.1 multiply_reduce_fusion
  10.5 0.1 reshape.217
  10.6 0.0 collective-permute-done
  10.6 1.7 %collective-permute-done.1 = bf16[64,1024]{1,0:T(8,128)(2,1)S(1)} collective-permute-done((bf16[64,1024]{1,0:T(8,128)(2,1)S(1)}, bf16[64,1024]{1,0:T(8,128)(2,1)S(1)}, u32[]{:S(2)}, u32[]{:S(2)}) %collective-permute-start.1) | collective-permute-done | bytes 131104 | tf_op jit(solution)/shard_map/ppermute | solution.py:371
  12.3 0.0 copy-done
  12.4 0.0 copy-done.2
  12.4 0.2 fusion.8
  12.5 1.3 %collective-permute-start.3 = (bf16[640,128]{1,0:T(8,128)(2,1)S(1)}, bf16[640,128]{1,0:T(8,128)(2,1)S(1)}, u32[]{:S(2)}, u32[]{:S(2)}) collective-permute-start(bf16[640,128]{1,0:T(8,128)(2,1)S(1)} %get-tuple-element.38), channel_id=1, source_target_pairs={{1,0},{2,1},{3,2},{4,3},{5,4},{6,5},{7,6},{8,7},{9,8},{10,9},{11,1... | collective-permute-start | bytes 491528 | tf_op jit(solution)/shard_map/ppermute | solution.py:371
  13.8 0.8 copy.19
  14.6 7.7 %all-to-all-start = ((s32[16,2,2]{2,1,0:T(2,128)}), s32[16,2,2]{2,1,0:T(2,128)S(1)}, u32[]{:S(2)}, u32[]{:S(2)}) async-start(s32[16,2,2]{2,1,0:T(2,128)} %copy.19), calls=%async_computation | async-start | bytes 32768 | tf_op jit(solution)/shard_map/all_to_all | solution.py:392
  22.3 3.3 %collective-permute-start.2 = (bf16[640,128]{1,0:T(8,128)(2,1)S(1)}, bf16[640,128]{1,0:T(8,128)(2,1)S(1)}, u32[]{:S(2)}, u32[]{:S(2)}) collective-permute-start(bf16[640,128]{1,0:T(8,128)(2,1)S(1)} %get-tuple-element.37), channel_id=1, source_target_pairs={{0,1},{1,2},{2,3},{3,4},{4,5},{5,6},{6,7},{7,8},{8,9},{9,10},{10,1... | collective-permute-start | bytes 491528 | tf_op jit(solution)/shard_map/ppermute | solution.py:371
  25.6 0.0 collective-permute-done.3
  25.6 0.1 fusion.20
  25.7 2.1 %collective-permute-done.2 = bf16[640,128]{1,0:T(8,128)(2,1)S(1)} collective-permute-done((bf16[640,128]{1,0:T(8,128)(2,1)S(1)}, bf16[640,128]{1,0:T(8,128)(2,1)S(1)}, u32[]{:S(2)}, u32[]{:S(2)}) %collective-permute-start.2) | collective-permute-done | bytes 163872 | tf_op jit(solution)/shard_map/ppermute | solution.py:371
  27.8 0.1 fusion.19
  28.0 0.4 pad_maximum_fusion.scene_ref
  28.4 0.3 all-to-all-done.requests
  28.7 7.6 %cut_windows.1 = bf16[32,288,128]{2,1,0:T(8,128)(2,1)} custom-call(s32[16,2,2]{2,1,0:T(2,128)S(1)} %all-to-all-done.requests, bf16[640,640]{1,0:T(8,128)(2,1)S(1)} %pad_maximum_fusion.scene_ref), custom_call_target="tpu_custom_call" | custom-call | tf_op jit(solution)/shard_map/cut_windows/pallas_call | solution.py:59
  36.3 0.0 copy-start.3
  36.3 7.0 %all-to-all-start.1 = ((bf16[16,576,128]{2,1,0:T(8,128)(2,1)}), bf16[16,576,128]{2,1,0:T(8,128)(2,1)S(1)}, u32[]{:S(2)}, u32[]{:S(2)}) async-start(bf16[16,576,128]{2,1,0:T(8,128)(2,1)} %bitcast.3), calls=%async_computation.1 | async-start | bytes 4718592 | tf_op jit(solution)/shard_map/all_to_all | solution.py:392
  43.4 0.0 copy-done.3
  43.4 0.4 pad_maximum_fusion.1.beside_ref
  43.8 0.0 copy-start.1
  43.8 0.9 copy-done.1
  44.7 13.4 %prepare.1 = (bf16[16,384,1280]{2,1,0:T(8,128)(2,1)}, bf16[16,256,1280]{2,1,0:T(8,128)(2,1)}, f32[16,8,256]{2,1,0:T(8,128)}) custom-call(bf16[512,512]{1,0:T(8,128)(2,1)S(1)} %copy-done, bf16[640,640]{1,0:T(8,128)(2,1)S(1)} %pad_maximum_fusion.1.beside_ref), custom_call_target="tpu_custom_call" | custom-call | flops 20000000000 | bytes 30000000 | tf_op jit(solution)/shard_map/prepare/pallas_call | solution.py:260
  58.1 22.9 %all-to-all-done.1 = bf16[16,576,128]{2,1,0:T(8,128)(2,1)S(1)} async-done(((bf16[16,576,128]{2,1,0:T(8,128)(2,1)}), bf16[16,576,128]{2,1,0:T(8,128)(2,1)S(1)}, u32[]{:S(2)}, u32[]{:S(2)}) %all-to-all-start.1) | async-done | bytes 2359328 | tf_op jit(solution)/shard_map/all_to_all | solution.py:392
  81.0 24.9 %surfaces.1 = (f32[16,22,256]{2,1,0:T(8,128)S(1)}, s32[1]{0:T(128)}) custom-call(s32[16]{0:T(128)S(1)} %multiply_add_fusion.slots, bf16[32,288,128]{2,1,0:T(8,128)(2,1)S(1)} %bitcast.33, bf16[16,384,1280]{2,1,0:T(8,128)(2,1)} %get-tuple-element.32.left_ref, bf16[16,256,1280]{2,1,0:T(8,128)(2,1)} %get-tuple-element.33.right_ref, ...), custom_call_target="tpu_custom_call" | custom-call | flops 20000000000 | bytes 30000000 | tf_op jit(solution)/shard_map/surfaces/pallas_call | solution.py:322
  106.5 0.1 copy.20
  106.7 0.3 reshape.220
  107.0 0.1 slice_bitcast_fusion
  107.2 0.3 copy.22
  107.5 0.2 reshape.222
  107.7 0.8 broadcast_multiply_fusion
  (9 shorter events, 0.1 us)
Async XLA Ops:
  0.0 12.4 %copy-start = (bf16[512,512]{1,0:T(8,128)(2,1)S(1)}, bf16[512,512]{1,0:T(8,128)(2,1)}, u32[]{:S(2)}) copy-start(bf16[512,512]{1,0:T(8,128)(2,1)} %first_ref.1) | copy-start | bytes 1572868
  0.0 12.4 %copy-start.2 = (bf16[512,512]{1,0:T(8,128)(2,1)S(1)}, bf16[512,512]{1,0:T(8,128)(2,1)}, u32[]{:S(2)}) copy-start(bf16[512,512]{1,0:T(8,128)(2,1)} %param.9) | copy-start | bytes 1572868
  1.1 9.5 %collective-permute-start = (bf16[64,1024]{1,0:T(8,128)(2,1)S(1)}, bf16[64,1024]{1,0:T(8,128)(2,1)S(1)}, u32[]{:S(2)}, u32[]{:S(2)}) collective-permute-start(bf16[64,1024]{1,0:T(8,128)(2,1)S(1)} %pad_maximum_fusion.6), channel_id=1, source_target_pairs={{0,16},{16,32},{32,48},{48,64},{64,80},{80,96},{96,112},{1,17},{17... | collective-permute-start | bytes 393224 | tf_op jit(solution)/shard_map/ppermute | solution.py:371
  6.0 6.3 %collective-permute-start.1 = (bf16[64,1024]{1,0:T(8,128)(2,1)S(1)}, bf16[64,1024]{1,0:T(8,128)(2,1)S(1)}, u32[]{:S(2)}, u32[]{:S(2)}) collective-permute-start(bf16[64,1024]{1,0:T(8,128)(2,1)S(1)} %pad_maximum_fusion.7), channel_id=1, source_target_pairs={{16,0},{32,16},{48,32},{64,48},{80,64},{96,80},{112,96},{17,1},{33... | collective-permute-start | bytes 393224 | tf_op jit(solution)/shard_map/ppermute | solution.py:371
  12.5 13.0 %collective-permute-start.3 = (bf16[640,128]{1,0:T(8,128)(2,1)S(1)}, bf16[640,128]{1,0:T(8,128)(2,1)S(1)}, u32[]{:S(2)}, u32[]{:S(2)}) collective-permute-start(bf16[640,128]{1,0:T(8,128)(2,1)S(1)} %get-tuple-element.38), channel_id=1, source_target_pairs={{1,0},{2,1},{3,2},{4,3},{5,4},{6,5},{7,6},{8,7},{9,8},{10,9},{11,1... | collective-permute-start | bytes 491528 | tf_op jit(solution)/shard_map/ppermute | solution.py:371
  14.6 14.1 %all-to-all-start = ((s32[16,2,2]{2,1,0:T(2,128)}), s32[16,2,2]{2,1,0:T(2,128)S(1)}, u32[]{:S(2)}, u32[]{:S(2)}) async-start(s32[16,2,2]{2,1,0:T(2,128)} %copy.19), calls=%async_computation | async-start | bytes 32768 | tf_op jit(solution)/shard_map/all_to_all | solution.py:392
  22.3 5.5 %collective-permute-start.2 = (bf16[640,128]{1,0:T(8,128)(2,1)S(1)}, bf16[640,128]{1,0:T(8,128)(2,1)S(1)}, u32[]{:S(2)}, u32[]{:S(2)}) collective-permute-start(bf16[640,128]{1,0:T(8,128)(2,1)S(1)} %get-tuple-element.37), channel_id=1, source_target_pairs={{0,1},{1,2},{2,3},{3,4},{4,5},{5,6},{6,7},{7,8},{8,9},{9,10},{10,1... | collective-permute-start | bytes 491528 | tf_op jit(solution)/shard_map/ppermute | solution.py:371
  36.3 7.0 %copy-start.3 = (s32[1,1,16]{2,1,0:T(1,128)S(1)}, s32[1,1,16]{2,1,0:T(1,128)}, u32[]{:S(2)}) copy-start(s32[1,1,16]{2,1,0:T(1,128)} %param.13) | copy-start | bytes 196
  36.3 44.6 %all-to-all-start.1 = ((bf16[16,576,128]{2,1,0:T(8,128)(2,1)}), bf16[16,576,128]{2,1,0:T(8,128)(2,1)S(1)}, u32[]{:S(2)}, u32[]{:S(2)}) async-start(bf16[16,576,128]{2,1,0:T(8,128)(2,1)} %bitcast.3), calls=%async_computation.1 | async-start | bytes 4718592 | tf_op jit(solution)/shard_map/all_to_all | solution.py:392
  43.8 0.9 copy-start.1
where the time goes:
time: 109 us; the launch traced here: 108 us
  Pallas kernels  45.9 us (42%)
  waiting for transfers between devices  27.1 us (25%)
  starting transfers between devices  26.1 us (24%)
  other arithmetic  4.37 us (4%)
  local copies, waits for them, and re-layouts  4.16 us (4%)
    pallas_call x1, Pallas kernels, surfaces_of(): pl.pallas_call(surface_kernel, grid=(17,), out_shape=[jax.ShapeDtypeStruc...  24.9 us
    all_to_all x2, waiting for transfers between devices, to_owners(): lax.all_to_all(values, 'strip', split_axis=0, concat_axis=0, tiled=True)  23.2 us
    all_to_all x2, starting transfers between devices, to_owners(): lax.all_to_all(values, 'strip', split_axis=0, concat_axis=0, tiled=True)  14.7 us
    pallas_call x1, Pallas kernels, prepared(): pl.pallas_call(prepare_kernel, grid=(16,), out_shape=[pltpu.HBM((16, m, n...  13.4 us
    ppermute x4, starting transfers between devices, moved(): return lax.ppermute(values, axis, pairs)  11.4 us
    pallas_call x1, Pallas kernels, cut_windows(): pl.pallas_call(cut_kernel, out_shape=jax.ShapeDtypeStruct((slots, PACKED,...  7.61 us
    ppermute x4, waiting for transfers between devices, moved(): return lax.ppermute(values, axis, pairs)  3.88 us
  transfers between devices with their start and end apart: 6, of which 4 were waited for; matrix products, arithmetic and copies ran while one was open for 4% of the time, Pallas kernels for 12%

commit v1 on v0

v1 whole, which is shorter than its diff:
```python
import functools

import jax
import jax.numpy as jnp
from jax import lax
from jax.experimental import pallas as pl
from jax.experimental.pallas import tpu as pltpu
from jax.sharding import PartitionSpec as P

SIDE = 128
SHIFTS = 64
SEARCH = 192
HALO = 64
EPSILON = 1e-05
COLS = 22
BANDS = 3
ROWS = 16
SPAN = 80
BLOCKS = SIDE // ROWS
DEPTH = BLOCKS + 2
PACKED = SEARCH + SEARCH // 2
EXTRA = 32
TALL = COLS * ROWS + EXTRA
DIMS = (((1,), (1,)), ((), ()))


def lane_iota(shape):
    return lax.broadcasted_iota(jnp.int32, shape, len(shape) - 1)


def cut_kernel(requests, scene_ref, out_ref, wide, *, place):
    for part in range(5):
        wide[part] = scene_ref[:, 128 * part : 128 * (part + 1)].astype(jnp.float32)
    wide[5] = jnp.zeros((640, 128), jnp.float32)
    lanes = lane_iota((SEARCH, 128))
    lower = lane_iota((SEARCH // 2, 128)) < 64

    def one(slot, carry):
        top = requests[slot, place, 0]
        left = requests[slot, place, 1]
        base = left // 128
        rest = left % 128
        turn = (128 - rest) % 128
        turned = [
            pltpu.roll(wide[base + part, pl.ds(top, SEARCH), :], turn, 1) for part in range(3)
        ]
        inside = lanes < 128 - rest
        near = jnp.where(inside, turned[0], turned[1])
        far = jnp.where(inside, turned[1], turned[2])
        out_ref[slot, :SEARCH, :] = near.astype(jnp.bfloat16)
        half = SEARCH // 2
        mixed = jnp.where(lower, far[:half], pltpu.roll(far[half:], 64, 1))
        out_ref[slot, SEARCH:, :] = mixed.astype(jnp.bfloat16)
        return carry

    lax.fori_loop(0, out_ref.shape[0], one, 0)


def cut_windows(scene, requests, place):
    slots = requests.shape[0]
    return pl.pallas_call(
        functools.partial(cut_kernel, place=place),
        out_shape=jax.ShapeDtypeStruct((slots, PACKED, 128), jnp.bfloat16),
        in_specs=[
            pl.BlockSpec(memory_space=pltpu.SMEM),
            pl.BlockSpec(memory_space=pltpu.VMEM),
        ],
        out_specs=pl.BlockSpec(memory_space=pltpu.VMEM),
        scratch_shapes=[pltpu.VMEM((6, 640, 128), jnp.float32)],
        compiler_params=pltpu.CompilerParams(vmem_limit_bytes=32 * 1024 * 1024),
        name="cut_windows",
    )(requests, scene)


def normalize(patch):
    centered = patch - jnp.mean(patch)
    return centered * lax.rsqrt(jnp.mean(centered * centered) + EPSILON)


def exchange(size):
    rows = lax.broadcasted_iota(jnp.int32, (size, size), 0)
    return (rows + lane_iota((size, size)) == size - 1).astype(jnp.bfloat16)


def halves(values):
    high = values.astype(jnp.bfloat16)
    low = (values - high.astype(jnp.float32)).astype(jnp.bfloat16)
    return high, low


def spread_template(values, left, row_at, lane_at, reverse):
    lanes = lane_iota((ROWS, 128)).astype(jnp.int16)
    groups = (lane_iota((ROWS, 128)) // 32).astype(jnp.int16)
    within = (lane_iota((ROWS, 128)) % 32).astype(jnp.int16)
    zero = jnp.zeros((ROWS, 128), jnp.bfloat16)
    blocks = [values[ROWS * q : ROWS * (q + 1)] for q in range(BLOCKS)]
    ends = []
    for group in range(2):
        end = zero
        for part in range(4):
            turned = pltpu.roll(blocks[4 * group + part], 32 * part, 1)
            end = jnp.where(groups == (part + 3) % 4, turned, end)
        ends.append(end)
    for a in range(COLS):
        shift = COLS - 1 - a if reverse else a
        rows = pl.ds(row_at + ROWS * a, ROWS)
        for q in range(BLOCKS):
            moved = pltpu.roll(blocks[q], shift, 1)
            moved = jnp.where(lanes >= shift, moved, zero)
            left[lane_at + q, rows] = moved
        for group in range(2):
            moved = pltpu.roll(ends[group], shift, 1)
            moved = jnp.where(within < shift, moved, zero)
            left[lane_at + BLOCKS + group, rows] = moved


def spread_window(near, far, right, lane_at, offsets):
    lanes = lane_iota((SEARCH, 128)).astype(jnp.int16)
    for b, offset in enumerate(offsets):
        back = (128 - offset) % 128
        main = near
        if offset:
            main = jnp.where(
                lanes < 128 - offset, pltpu.roll(near, back, 1), pltpu.roll(far, back, 1)
            )
        rows = pl.ds(SPAN * b, SPAN)
        for q in range(BLOCKS):
            right[lane_at + q, rows] = main[ROWS * q : ROWS * q + SPAN]
        turned = [pltpu.roll(far, (back + 32 * part) % 128, 1) for part in range(4)]
        few = (lane_iota((SPAN, 128)) // 32).astype(jnp.int16)
        for group in range(2):
            tail = turned[0][ROWS * 4 * group : ROWS * 4 * group + SPAN]
            for part in range(1, 4):
                q = 4 * group + part
                tail = jnp.where(few == part, turned[part][ROWS * q : ROWS * q + SPAN], tail)
            right[lane_at + BLOCKS + group, rows] = tail


def fold_diagonals(product, hold):
    for half in range(2):
        hold[half, : COLS * ROWS] = product[:, 128 * half : 128 * (half + 1)]
    groups = []
    for group in range(3):
        terms = [
            jnp.concatenate(
                [hold[half, pl.ds(128 * group + p, 8, stride=ROWS), :] for half in range(2)], axis=1
            )
            for p in range(ROWS)
        ]
        for step in (8, 4, 2, 1):
            terms = [terms[p] + pltpu.roll(terms[p + step], 256 - step, 1) for p in range(step)]
        groups.append(terms[0])
    return jnp.concatenate(groups, axis=0)


def multiplied(left, right):
    factors = [
        jnp.concatenate([side[block] for block in range(side.shape[0])], axis=1)
        for side in (left, right)
    ]
    return lax.dot_general(*factors, DIMS, preferred_element_type=jnp.float32)


def search_block(windows_ref, slot):
    near = windows_ref[slot, :SEARCH, :]
    packed = windows_ref[slot, SEARCH:, :]
    return near, jnp.concatenate([packed, pltpu.roll(packed, 64, 1)], axis=0)


def flipped_centre(near, far):
    flip = exchange(128)
    low, high = [
        jnp.dot(flip, part[32:160], preferred_element_type=jnp.float32) for part in (near, far)
    ]
    lanes = lane_iota((128, 128))
    return jnp.where(lanes < 96, pltpu.roll(low, 96, 1), pltpu.roll(high, 96, 1))


def flipped_around(beside_ref, row, col):
    return jnp.dot(
        exchange(SEARCH),
        beside_ref[pl.ds(row + 32, SEARCH), pl.ds(col, 256)],
        preferred_element_type=jnp.float32,
    ).astype(jnp.bfloat16)


def place_of(patch):
    return pl.multiple_of(patch // 4 * 128, 128), pl.multiple_of(patch % 4 * 128, 128)


def careful_kernel(owners, later, first_ref, beside_ref, windows_ref, others_ref, out_ref, left, right, hold):
    right[:, SPAN * BANDS :] = jnp.zeros((2 * DEPTH, 256 - SPAN * BANDS, 128), jnp.bfloat16)
    count = COLS * ROWS

    hold[:, count:] = jnp.zeros((2, 32, 128), jnp.float32)
    out_ref[16] = jnp.zeros((24, 256), jnp.float32)

    def one(patch, carry):
        row, col = place_of(patch)
        near, far = [
            jnp.where(later[patch] > 0, other, one)
            for one, other in zip(
                search_block(windows_ref, owners[patch]), search_block(others_ref, owners[patch])
            )
        ]
        template = normalize(first_ref[pl.ds(row, 128), pl.ds(col, 128)].astype(jnp.float32))
        centre = flipped_centre(near, far)
        around = flipped_around(beside_ref, row, col)
        inner = first_ref[pl.ds(row, 128), pl.ds(col, 128)].astype(jnp.float32)
        sides = ((template, jnp.mean(centre), False), (normalize(centre), jnp.mean(inner), True))
        rest = jnp.float32(0.0)
        for place, (values, level, reverse) in enumerate(sides):
            high, low = halves(values)
            for half, piece in enumerate((high, low)):
                spread_template(piece, left, count * half, DEPTH * place, reverse)
            rest += level * (
                jnp.sum(high.astype(jnp.float32)) + jnp.sum(low.astype(jnp.float32))
            )
        spread_window(near, far, right, 0, (0, 22, 44))
        spread_window(around[:, :128], around[:, 128:], right, DEPTH, (75, 53, 31))
        both = multiplied(left, right)
        out_ref[patch] = fold_diagonals(both[:count] + both[count:], hold) - rest
        return carry

    lax.fori_loop(0, 16, one, 0)


def careful_surfaces(owners, later, first, beside, windows, others):
    return pl.pallas_call(
        careful_kernel,
        out_shape=jax.ShapeDtypeStruct((17, 24, 256), jnp.float32),
        in_specs=[pl.BlockSpec(memory_space=pltpu.SMEM)] * 2
        + [pl.BlockSpec(memory_space=pltpu.VMEM)] * 4,
        out_specs=pl.BlockSpec(memory_space=pltpu.VMEM),
        scratch_shapes=[
            pltpu.VMEM((2 * DEPTH, 2 * COLS * ROWS, 128), jnp.bfloat16),
            pltpu.VMEM((2 * DEPTH, 256, 128), jnp.bfloat16),
            pltpu.VMEM((2, 384, 128), jnp.float32),
        ],
        compiler_params=pltpu.CompilerParams(vmem_limit_bytes=40 * 1024 * 1024),
        name="careful_surfaces",
    )(owners, later, first, beside, windows, others)


def ones_rows(left, reverse):
    index = lax.broadcasted_iota(jnp.int32, (EXTRA, 128), 0)
    lanes = lane_iota((EXTRA, 128))
    shift = COLS - 1 - index if reverse else index
    main = jnp.where((index < COLS) & (lanes >= shift), 1.0, 0.0).astype(jnp.bfloat16)
    tail = jnp.where((index < COLS) & (lanes % 32 < shift), 1.0, 0.0).astype(jnp.bfloat16)
    for q in range(BLOCKS):
        left[q, COLS * ROWS :] = main
    for group in range(2):
        left[BLOCKS + group, COLS * ROWS :] = tail


def level_of(values):
    mean = jnp.mean(values)
    centered = values - mean
    spread = jnp.mean(centered * centered)
    large = jnp.where(mean * mean > 4.0 * spread, 1.0, 0.0)
    return mean, lax.rsqrt(jnp.full((1, 256), spread + EPSILON)), large


def surface_kernel(
    owners, turns, count_of, first_ref, beside_ref, windows_ref, *rest, phase
):
    before, (out_ref, large_ref, *scratch) = (rest[0], rest[1:]) if phase else (None, rest)
    count = COLS * ROWS
    large_ref[0] = 0
    if phase:
        out_ref[...] = before[...]
    for ahead, behind, front, back, side, hold in (scratch[:6], scratch[6:]):
        hold[:, count:] = jnp.zeros((2, 32, 128), jnp.float32)
        ones_rows(front, False)
        ones_rows(back, True)
        for right in (ahead, behind):
            right[:, SPAN * BANDS :] = jnp.zeros((DEPTH, 256 - SPAN * BANDS, 128), jnp.bfloat16)

    def build(index, buffers):
        ahead, behind, front, back, side, hold = buffers
        patch = turns[index]
        row, col = place_of(patch)
        near, far = search_block(windows_ref, owners[patch])
        tile = first_ref[pl.ds(row, 128), pl.ds(col, 128)]
        spread_window(near, far, ahead, 0, (0, 22, 44))
        spread_template(tile, front, 0, 0, False)
        centre = flipped_centre(near, far)
        spread_template(centre.astype(jnp.bfloat16), back, 0, 0, True)
        around = flipped_around(beside_ref, row, col)
        spread_window(around[:, :128], around[:, 128:], behind, 0, (75, 53, 31))
        bad = jnp.float32(0.0)
        for place, values in enumerate((tile.astype(jnp.float32), centre)):
            mean, scale, large = level_of(values)
            side[2 * place : 2 * place + 1, :] = scale * mean
            side[2 * place + 1 : 2 * place + 2, :] = scale
            bad = jnp.maximum(bad, large)
        large_ref[0] = jnp.maximum(large_ref[0], bad.astype(jnp.int32))

    def sums(index, buffers):
        ahead, behind, front, back, side, hold = buffers
        one = multiplied(front, ahead)
        two = multiplied(back, behind)
        raw = side[1:2, :] * one[:count] + side[3:4, :] * two[:count]
        box = side[0:1, :] * one[count:] + side[2:3, :] * two[count:]
        for shift in (1, 2, 4, 8):
            box = box + pltpu.roll(box, 256 - shift, 1)
        patch = jnp.where(index < count_of[0], turns[jnp.minimum(index, 15)], 16)
        out_ref[patch] = fold_diagonals(raw, hold) - box[:24]

    build(0, scratch[:6])

    def pair(step, carry):
        sums(2 * step, scratch[:6])
        build(jnp.minimum(2 * step + 1, 15), scratch[6:])
        sums(2 * step + 1, scratch[6:])
        build(jnp.minimum(2 * step + 2, 15), scratch[:6])
        return carry

    lax.fori_loop(0, (count_of[0] + 1) // 2, pair, 0)


def surfaces_of(owners, turns, count_of, first, beside, windows, before=None):
    phase = int(before is not None)
    arrays = [first, beside, windows] + [before] * phase
    factors = [pltpu.VMEM((DEPTH, 256, 128), jnp.bfloat16)] * 2
    factors += [pltpu.VMEM((DEPTH, TALL, 128), jnp.bfloat16)] * 2
    sides = [pltpu.VMEM((8, 256), jnp.float32), pltpu.VMEM((2, 384, 128), jnp.float32)]
    return pl.pallas_call(
        functools.partial(surface_kernel, phase=phase),
        out_shape=[
            jax.ShapeDtypeStruct((17, 24, 256), jnp.float32),
            jax.ShapeDtypeStruct((1,), jnp.int32),
        ],
        in_specs=[pl.BlockSpec(memory_space=pltpu.SMEM)] * 3
        + [pl.BlockSpec(memory_space=pltpu.VMEM)] * len(arrays),
        out_specs=[
            pl.BlockSpec(memory_space=pltpu.VMEM),
            pl.BlockSpec(memory_space=pltpu.SMEM),
        ],
        scratch_shapes=(factors + sides) * 2,
        compiler_params=pltpu.CompilerParams(vmem_limit_bytes=32 * 1024 * 1024),
        cost_estimate=pl.CostEstimate(
            flops=20_000_000_000, bytes_accessed=8_000_000, transcendentals=0
        ),
        name=("surfaces_later" if phase else "surfaces_early"),
    )(owners, turns, count_of, *arrays)


def finish(folded, mask):
    parts = folded[:16, :COLS, : SPAN * BANDS].reshape(16, COLS, BANDS, SPAN)[..., :SHIFTS]
    surface = parts.transpose(0, 3, 2, 1).reshape(16, SHIFTS, BANDS * COLS)[:, :, :SHIFTS]
    scale = mask.reshape(16, 1).astype(jnp.float32) / (2.0 * SIDE)
    return surface.reshape(16, SHIFTS * SHIFTS) * scale


def moved(values, axis, forward):
    count = lax.axis_size(axis)
    pairs = [(i, i + 1) if forward else (i + 1, i) for i in range(count - 1)]
    return lax.ppermute(values, axis, pairs)


def rows_around(first, second):
    from_above = moved(jnp.concatenate([first[-HALO:], second[-HALO:]], 1), "band", True)
    from_below = moved(jnp.concatenate([first[:HALO], second[:HALO]], 1), "band", False)
    return from_above, from_below


def with_margins(first, second, from_above, from_below):
    width = first.shape[1]
    first = jnp.concatenate([from_above[:, :width], first, from_below[:, :width]], 0)
    second = jnp.concatenate([from_above[:, width:], second, from_below[:, width:]], 0)
    from_left = moved(jnp.concatenate([first[:, -HALO:], second[:, -HALO:]], 1), "strip", True)
    from_right = moved(jnp.concatenate([first[:, :HALO], second[:, :HALO]], 1), "strip", False)
    first = jnp.concatenate([from_left[:, :HALO], first, from_right[:, :HALO]], 1)
    second = jnp.concatenate([from_left[:, HALO:], second, from_right[:, HALO:]], 1)
    return first, second


def to_owners(values):
    return lax.all_to_all(values, "strip", split_axis=0, concat_axis=0, tiled=True)


def on_device(first, second, owner_strip, target_tile, offsets, valid_mask):
    strips = lax.axis_size("strip")
    from_above, from_below = rows_around(first, second)
    order = jnp.arange(16, dtype=jnp.int32)
    owners = owner_strip.reshape(16)
    earlier = (owners[:, None] == owners[None, :]) & (order[None, :] < order[:, None])
    later = jnp.sum(earlier.astype(jnp.int32), axis=1)
    slot_of = owners * 2 + later
    placing = (slot_of[:, None] == jnp.arange(2 * strips, dtype=jnp.int32)[None, :]).astype(jnp.int32)
    tiles = target_tile.reshape(16)
    shifts = offsets.reshape(16, 2)
    corner = jnp.stack(
        [tiles // 4 * SIDE + shifts[:, 0] + 32, tiles % 4 * SIDE + shifts[:, 1] + 32], axis=1
    )
    outgoing = jnp.sum(placing[:, :, None] * corner[:, None, :], axis=0).reshape(strips, 2, 2)
    outgoing, from_above, from_below = lax.optimization_barrier((outgoing, from_above, from_below))
    requests = to_owners(outgoing)
    beside, wide = with_margins(first, second, from_above, from_below)
    windows = [to_owners(cut_windows(wide, requests, place)) for place in range(2)]
    ahead = (later[None, :] < later[:, None]) | (
        (later[None, :] == later[:, None]) & (order[None, :] < order[:, None])
    )
    rank = jnp.sum(ahead.astype(jnp.int32), axis=1)
    late = jnp.sum(later).reshape(1)
    early = 16 - late
    turns, later_turns = [
        jnp.sum((rank[None, :] == (order + at)[:, None]).astype(jnp.int32) * order[None, :], axis=1)
        for at in (0, early)
    ]
    folded, large = surfaces_of(owners, turns, early, first, beside, windows[0])
    folded, larger = surfaces_of(owners, later_turns, late, first, beside, windows[1], folded)
    folded = lax.cond(
        jnp.maximum(large[0], larger[0]) > 0,
        lambda: careful_surfaces(owners, later, first, beside, *windows),
        lambda: folded,
    )
    return finish(folded, valid_mask).reshape(1, 1, 16, SHIFTS * SHIFTS)


def solution(mesh):
    return jax.shard_map(
        on_device,
        mesh=mesh,
        in_specs=(
            P("band", "strip"),
            P("band", "strip"),
            P("band", "strip", None, None),
            P("band", "strip", None),
            P("band", "strip", None, None),
            P("band", "strip", None),
        ),
        out_specs=P("band", "strip", None, None),
        check_vma=False,
    )
```

time: 109 us -> 95.8 us (0.88)
  waiting for transfers between devices: 27.1 us -> 16.3 us
  Pallas kernels: 45.9 us -> 38.5 us
  starting transfers between devices: 26.1 us -> 27.7 us
  between operations: 0.87 us -> 2.41 us
    pallas_call x3 -> x4, Pallas kernels: 45.9 us -> 38.5 us  [the longest x2 29.3 us: surfaces_of(): pl.pallas_call(functools.partial(surface_kernel, phase=phase), out_shape=...]
    all_to_all x2 -> x3, waiting for transfers between devices: 23.2 us -> 16.3 us  [to_owners(): lax.all_to_all(values, 'strip', split_axis=0, concat_axis=0, tiled=True)]
    ppermute x4, waiting for transfers between devices: 3.88 us -> 0.01 us  [moved(): return lax.ppermute(values, axis, pairs)]
    all_to_all x2 -> x3, starting transfers between devices: 14.7 us -> 16.5 us  [to_owners(): lax.all_to_all(values, 'strip', split_axis=0, concat_axis=0, tiled=True)]
  transfers between devices with their start and end apart: 6 -> 7, of which waited for: 4 -> 2; matrix products, arithmetic and copies ran while one was open for 4% -> 6% of each run, Pallas kernels for 12% -> 29%
where the time goes in v1:
time: 95.8 us; the launch traced here: 94.4 us
  Pallas kernels  38.5 us (40%)
  starting transfers between devices  27.7 us (29%)
  waiting for transfers between devices  16.3 us (17%)
  other arithmetic  5.34 us (6%)
  local copies, waits for them, and re-layouts  3.91 us (4%)
  between operations  2.41 us (3%)
    pallas_call x2, Pallas kernels, surfaces_of(): pl.pallas_call(functools.partial(surface_kernel, phase=phase), out_shape=...  29.3 us
    all_to_all x3, starting transfers between devices, to_owners(): lax.all_to_all(values, 'strip', split_axis=0, concat_axis=0, tiled=True)  16.5 us
    all_to_all x3, waiting for transfers between devices, to_owners(): lax.all_to_all(values, 'strip', split_axis=0, concat_axis=0, tiled=True)  16.3 us
    ppermute x4, starting transfers between devices, moved(): return lax.ppermute(values, axis, pairs)  11.3 us
    pallas_call x2, Pallas kernels, cut_windows(): pl.pallas_call(functools.partial(cut_kernel, place=place), out_shape=jax....  9.21 us
  transfers between devices with their start and end apart: 7, of which 2 were waited for; matrix products, arithmetic and copies ran while one was open for 6% of the time, Pallas kernels for 29%

profile of v1, /device:TPU:1, one launch (start us, length us, event | category | flops | bytes accessed | tf_op | source)
XLA Modules:
  0.0 94.4 jit_solution(5767947224314893096)
XLA Ops:
  0.0 0.0 copy-start
  0.0 0.0 copy-start.1
  0.0 1.0 %fusion.19 = (bf16[64,512]{1,0:T(8,128)(2,1)S(1)}, bf16[64,512]{1,0:T(8,128)(2,1)S(1)}, bf16[64,512]{1,0:T(8,128)(2,1)S(1)}, bf16[64,512]{1,0:T(8,128)(2,1)S(1)}) fusion(bf16[512,512]{1,0:T(8,128)(2,1)} %first_ref.3, bf16[512,512]{1,0:T(8,128)(2,1)} %param.9), kind=kLoop, calls=%fused_computation.51 | loop fusion | bytes 524288 | tf_op jit(solution)/shard_map/slice | solution.py:365
  1.1 3.3 %collective-permute-start.1 = (bf16[64,1024]{1,0:T(8,128)(2,1)S(1)}, bf16[64,1024]{1,0:T(8,128)(2,1)S(1)}, u32[]{:S(2)}, u32[]{:S(2)}) collective-permute-start(bf16[64,1024]{1,0:T(8,128)(2,1)S(1)} %pad_maximum_fusion.7), channel_id=1, source_target_pairs={{16,0},{32,16},{48,32},{64,48},{80,64},{96,80},{112,96},{17,1},{33... | collective-permute-start | bytes 393224 | tf_op jit(solution)/shard_map/ppermute | solution.py:360
  4.4 3.5 %collective-permute-start = (bf16[64,1024]{1,0:T(8,128)(2,1)S(1)}, bf16[64,1024]{1,0:T(8,128)(2,1)S(1)}, u32[]{:S(2)}, u32[]{:S(2)}) collective-permute-start(bf16[64,1024]{1,0:T(8,128)(2,1)S(1)} %pad_maximum_fusion.6), channel_id=1, source_target_pairs={{0,16},{16,32},{32,48},{48,64},{64,80},{80,96},{96,112},{1,17},{17... | collective-permute-start | bytes 393224 | tf_op jit(solution)/shard_map/ppermute | solution.py:360
  8.0 1.5 %convert_reduce_fusion = (s32[]{:T(128)}, s32[16]{0:T(128)S(1)}) fusion(s32[16]{0:T(128)} %bitcast.33), kind=kLoop, calls=%fused_computation.25 | loop fusion | flops 1519 | bytes 132 | tf_op jit(solution)/shard_map/reduce_sum | solution.py:407
  9.5 0.7 multiply_add_fusion
  10.1 0.1 fusion.15
  10.2 0.8 add_add_fusion
  11.0 0.1 multiply_reduce_fusion
  11.1 0.1 reshape.223
  11.2 0.0 collective-permute-done.1
  11.2 0.0 collective-permute-done
  11.2 0.0 copy-start.3
  11.2 0.0 copy-start.5
  11.2 0.0 copy-done
  11.3 0.0 copy-done.1
  11.3 0.2 fusion.8
  11.4 3.1 %collective-permute-start.2 = (bf16[640,128]{1,0:T(8,128)(2,1)S(1)}, bf16[640,128]{1,0:T(8,128)(2,1)S(1)}, u32[]{:S(2)}, u32[]{:S(2)}) collective-permute-start(bf16[640,128]{1,0:T(8,128)(2,1)S(1)} %get-tuple-element.45), channel_id=1, source_target_pairs={{0,1},{1,2},{2,3},{3,4},{4,5},{5,6},{6,7},{7,8},{8,9},{9,10},{10,1... | collective-permute-start | bytes 491528 | tf_op jit(solution)/shard_map/ppermute | solution.py:360
  14.6 0.0 copy-done.3
  14.6 0.0 copy-done.5
  14.6 1.3 %collective-permute-start.3 = (bf16[640,128]{1,0:T(8,128)(2,1)S(1)}, bf16[640,128]{1,0:T(8,128)(2,1)S(1)}, u32[]{:S(2)}, u32[]{:S(2)}) collective-permute-start(bf16[640,128]{1,0:T(8,128)(2,1)S(1)} %get-tuple-element.46), channel_id=1, source_target_pairs={{1,0},{2,1},{3,2},{4,3},{5,4},{6,5},{7,6},{8,7},{9,8},{10,9},{11,1... | collective-permute-start | bytes 491528 | tf_op jit(solution)/shard_map/ppermute | solution.py:360
  15.9 0.8 copy.19
  16.7 7.6 %all-to-all-start = ((s32[16,2,2]{2,1,0:T(2,128)}), s32[16,2,2]{2,1,0:T(2,128)S(1)}, u32[]{:S(2)}, u32[]{:S(2)}) async-start(s32[16,2,2]{2,1,0:T(2,128)} %copy.19), calls=%async_computation | async-start | bytes 32768 | tf_op jit(solution)/shard_map/all_to_all | solution.py:381
  24.3 0.0 collective-permute-done.2
  24.3 0.1 fusion.21
  24.4 0.0 collective-permute-done.3
  24.4 0.7 fusion.22
  25.2 0.4 pad_maximum_fusion.1.scene_ref
  25.6 5.2 %all-to-all-done.requests = s32[16,2,2]{2,1,0:T(2,128)S(1)} async-done(((s32[16,2,2]{2,1,0:T(2,128)}), s32[16,2,2]{2,1,0:T(2,128)S(1)}, u32[]{:S(2)}, u32[]{:S(2)}) %all-to-all-start) | async-done | bytes 288 | tf_op jit(solution)/shard_map/all_to_all | solution.py:381
  30.8 4.6 %cut_windows.2 = bf16[16,288,128]{2,1,0:T(8,128)(2,1)} custom-call(s32[16,2,2]{2,1,0:T(2,128)S(1)} %all-to-all-done.requests, bf16[640,640]{1,0:T(8,128)(2,1)S(1)} %pad_maximum_fusion.1.scene_ref), custom_call_target="tpu_custom_call" | custom-call | tf_op jit(solution)/shard_map/cut_windows/pallas_call | solution.py:61
  35.4 0.0 copy-start.8
  35.4 3.8 %all-to-all-start.1 = ((bf16[16,288,128]{2,1,0:T(8,128)(2,1)}), bf16[16,288,128]{2,1,0:T(8,128)(2,1)S(1)}, u32[]{:S(2)}, u32[]{:S(2)}) async-start(bf16[16,288,128]{2,1,0:T(8,128)(2,1)} %cut_windows.2), calls=%async_computation.1 | async-start | bytes 2359296 | tf_op jit(solution)/shard_map/all_to_all | solution.py:381
  39.2 0.0 copy-start.2
  39.2 0.0 copy-start.4
  39.2 0.0 copy-start.6
  40.0 0.2 convert_reduce_fusion.2
  40.2 0.2 select_reduce_fusion
  40.3 0.0 copy-done.8
  40.4 4.6 %cut_windows.3 = bf16[16,288,128]{2,1,0:T(8,128)(2,1)} custom-call(s32[16,2,2]{2,1,0:T(2,128)S(1)} %all-to-all-done.requests, bf16[640,640]{1,0:T(8,128)(2,1)S(1)} %pad_maximum_fusion.1.scene_ref), custom_call_target="tpu_custom_call" | custom-call | tf_op jit(solution)/shard_map/cut_windows/pallas_call | solution.py:61
  45.0 0.0 copy-done.2
  45.0 0.0 copy-done.4
  45.0 0.0 copy-done.6
  45.0 0.4 pad_maximum_fusion.beside_ref
  45.4 0.0 copy-start.7
  45.4 11.1 %all-to-all-done.1.windows_ref = bf16[16,288,128]{2,1,0:T(8,128)(2,1)S(1)} async-done(((bf16[16,288,128]{2,1,0:T(8,128)(2,1)}), bf16[16,288,128]{2,1,0:T(8,128)(2,1)S(1)}, u32[]{:S(2)}, u32[]{:S(2)}) %all-to-all-start.1) | async-done | bytes 1179680 | tf_op jit(solution)/shard_map/all_to_all | solution.py:381
  56.6 5.0 %all-to-all-start.2 = ((bf16[16,288,128]{2,1,0:T(8,128)(2,1)}), bf16[16,288,128]{2,1,0:T(8,128)(2,1)}, u32[]{:S(2)}, u32[]{:S(2)}) async-start(bf16[16,288,128]{2,1,0:T(8,128)(2,1)} %cut_windows.3), calls=%async_computation.2 | async-start | bytes 2359296 | tf_op jit(solution)/shard_map/all_to_all | solution.py:381
  61.6 0.0 copy-done.7
  61.6 22.7 %surfaces_early.1 = (f32[17,24,256]{2,1,0:T(8,128)S(1)}, s32[1]{0:T(128)}) custom-call(s32[16]{0:T(128)S(1)} %bitcast.34, s32[16]{0:T(128)S(1)} %get-tuple-element.42.turns, s32[1]{0:T(128)} %sub.7.count_of, bf16[512,512]{1,0:T(8,128)(2,1)S(1)} %copy-done, bf16[640,640]{1,0:T(8,128)(2,1)S(1)} %pad_maximum_fusion.beside_ref, ...), custom_call_target="tpu_custom_call" | custom-call | flops 20000000000 | bytes 8000000 | tf_op jit(solution)/shard_map/surfaces_early/pallas_call | solution.py:329
  84.3 0.0 all-to-all-done.2.windows_ref
  84.3 6.7 %surfaces_later.1 = (f32[17,24,256]{2,1,0:T(8,128)S(1)}, s32[1]{0:T(128)}) custom-call(s32[16]{0:T(128)S(1)} %bitcast.35, s32[16]{0:T(128)S(1)} %get-tuple-element.41.turns, s32[1]{0:T(128)} %bitcast.1.count_of, bf16[512,512]{1,0:T(8,128)(2,1)S(1)} %copy-done, bf16[640,640]{1,0:T(8,128)(2,1)S(1)} %pad_maximum_fusion.beside_ref, ...), custom_call_target="tpu_custom_call" | custom-call | flops 20000000000 | bytes 8000000 | tf_op jit(solution)/shard_map/surfaces_later/pallas_call | solution.py:329
  92.2 0.2 conditional.1
  92.5 0.1 copy.20
  92.6 0.3 reshape.224
  92.9 0.1 slice_bitcast_fusion
  93.2 0.3 copy.22
  93.4 0.2 reshape.226
  93.6 0.8 broadcast_multiply_fusion
  (10 shorter events, 0.2 us)
Async XLA Ops:
  0.0 11.2 %copy-start = (bf16[512,512]{1,0:T(8,128)(2,1)S(1)}, bf16[512,512]{1,0:T(8,128)(2,1)}, u32[]{:S(2)}) copy-start(bf16[512,512]{1,0:T(8,128)(2,1)} %first_ref.3) | copy-start | bytes 1572868
  0.0 11.3 %copy-start.1 = (bf16[512,512]{1,0:T(8,128)(2,1)S(1)}, bf16[512,512]{1,0:T(8,128)(2,1)}, u32[]{:S(2)}) copy-start(bf16[512,512]{1,0:T(8,128)(2,1)} %param.9) | copy-start | bytes 1572868
  1.1 10.1 %collective-permute-start.1 = (bf16[64,1024]{1,0:T(8,128)(2,1)S(1)}, bf16[64,1024]{1,0:T(8,128)(2,1)S(1)}, u32[]{:S(2)}, u32[]{:S(2)}) collective-permute-start(bf16[64,1024]{1,0:T(8,128)(2,1)S(1)} %pad_maximum_fusion.7), channel_id=1, source_target_pairs={{16,0},{32,16},{48,32},{64,48},{80,64},{96,80},{112,96},{17,1},{33... | collective-permute-start | bytes 393224 | tf_op jit(solution)/shard_map/ppermute | solution.py:360
  4.4 6.8 %collective-permute-start = (bf16[64,1024]{1,0:T(8,128)(2,1)S(1)}, bf16[64,1024]{1,0:T(8,128)(2,1)S(1)}, u32[]{:S(2)}, u32[]{:S(2)}) collective-permute-start(bf16[64,1024]{1,0:T(8,128)(2,1)S(1)} %pad_maximum_fusion.6), channel_id=1, source_target_pairs={{0,16},{16,32},{32,48},{48,64},{64,80},{80,96},{96,112},{1,17},{17... | collective-permute-start | bytes 393224 | tf_op jit(solution)/shard_map/ppermute | solution.py:360
  11.2 3.4 %copy-start.3 = (bf16[64,512]{1,0:T(8,128)(2,1)}, bf16[64,512]{1,0:T(8,128)(2,1)S(1)}, u32[]{:S(2)}) copy-start(bf16[64,512]{1,0:T(8,128)(2,1)S(1)} %get-tuple-element.55) | copy-start | bytes 196612
  11.2 3.3 %copy-start.5 = (bf16[64,512]{1,0:T(8,128)(2,1)}, bf16[64,512]{1,0:T(8,128)(2,1)S(1)}, u32[]{:S(2)}) copy-start(bf16[64,512]{1,0:T(8,128)(2,1)S(1)} %get-tuple-element.57) | copy-start | bytes 196612
  11.4 12.9 %collective-permute-start.2 = (bf16[640,128]{1,0:T(8,128)(2,1)S(1)}, bf16[640,128]{1,0:T(8,128)(2,1)S(1)}, u32[]{:S(2)}, u32[]{:S(2)}) collective-permute-start(bf16[640,128]{1,0:T(8,128)(2,1)S(1)} %get-tuple-element.45), channel_id=1, source_target_pairs={{0,1},{1,2},{2,3},{3,4},{4,5},{5,6},{6,7},{7,8},{8,9},{9,10},{10,1... | collective-permute-start | bytes 491528 | tf_op jit(solution)/shard_map/ppermute | solution.py:360
  14.6 9.9 %collective-permute-start.3 = (bf16[640,128]{1,0:T(8,128)(2,1)S(1)}, bf16[640,128]{1,0:T(8,128)(2,1)S(1)}, u32[]{:S(2)}, u32[]{:S(2)}) collective-permute-start(bf16[640,128]{1,0:T(8,128)(2,1)S(1)} %get-tuple-element.46), channel_id=1, source_target_pairs={{1,0},{2,1},{3,2},{4,3},{5,4},{6,5},{7,6},{8,7},{9,8},{10,9},{11,1... | collective-permute-start | bytes 491528 | tf_op jit(solution)/shard_map/ppermute | solution.py:360
  16.7 14.1 %all-to-all-start = ((s32[16,2,2]{2,1,0:T(2,128)}), s32[16,2,2]{2,1,0:T(2,128)S(1)}, u32[]{:S(2)}, u32[]{:S(2)}) async-start(s32[16,2,2]{2,1,0:T(2,128)} %copy.19), calls=%async_computation | async-start | bytes 32768 | tf_op jit(solution)/shard_map/all_to_all | solution.py:381
  35.4 5.0 %copy-start.8 = (s32[1,1,16]{2,1,0:T(1,128)S(1)}, s32[1,1,16]{2,1,0:T(1,128)}, u32[]{:S(2)}) copy-start(s32[1,1,16]{2,1,0:T(1,128)} %param.13) | copy-start | bytes 196
  35.4 21.2 %all-to-all-start.1 = ((bf16[16,288,128]{2,1,0:T(8,128)(2,1)}), bf16[16,288,128]{2,1,0:T(8,128)(2,1)S(1)}, u32[]{:S(2)}, u32[]{:S(2)}) async-start(bf16[16,288,128]{2,1,0:T(8,128)(2,1)} %cut_windows.2), calls=%async_computation.1 | async-start | bytes 2359296 | tf_op jit(solution)/shard_map/all_to_all | solution.py:381
  39.2 5.8 %copy-start.2 = (bf16[640,64]{1,0:T(8,128)(2,1)S(1)}, bf16[640,64]{1,0:T(8,128)(2,1)}, u32[]{:S(2)}) copy-start(bf16[640,64]{1,0:T(8,128)(2,1)} %get-tuple-element.54) | copy-start | bytes 245764
  39.2 5.8 %copy-start.4 = (bf16[64,512]{1,0:T(8,128)(2,1)S(1)}, bf16[64,512]{1,0:T(8,128)(2,1)}, u32[]{:S(2)}) copy-start(bf16[64,512]{1,0:T(8,128)(2,1)} %copy-done.3) | copy-start | bytes 196612
  39.2 5.7 %copy-start.6 = (bf16[64,512]{1,0:T(8,128)(2,1)S(1)}, bf16[64,512]{1,0:T(8,128)(2,1)}, u32[]{:S(2)}) copy-start(bf16[64,512]{1,0:T(8,128)(2,1)} %copy-done.5) | copy-start | bytes 196612
  45.4 16.2 %copy-start.7 = (s32[1,1,16,1]{2,3,1,0:T(1,128)S(1)}, s32[1,1,16,1]{2,3,1,0:T(1,128)}, u32[]{:S(2)}) copy-start(s32[1,1,16,1]{2,3,1,0:T(1,128)} %param.10) | copy-start | bytes 196
  56.6 27.7 %all-to-all-start.2 = ((bf16[16,288,128]{2,1,0:T(8,128)(2,1)}), bf16[16,288,128]{2,1,0:T(8,128)(2,1)}, u32[]{:S(2)}, u32[]{:S(2)}) async-start(bf16[16,288,128]{2,1,0:T(8,128)(2,1)} %cut_windows.3), calls=%async_computation.2 | async-start | bytes 2359296 | tf_op jit(solution)/shard_map/all_to_all | solution.py:381

commit v2 on v1

--- a/solution.py
+++ b/solution.py
@@ -396,8 +396,7 @@
         [tiles // 4 * SIDE + shifts[:, 0] + 32, tiles % 4 * SIDE + shifts[:, 1] + 32], axis=1
     )
     outgoing = jnp.sum(placing[:, :, None] * corner[:, None, :], axis=0).reshape(strips, 2, 2)
-    outgoing, from_above, from_below = lax.optimization_barrier((outgoing, from_above, from_below))
-    requests = to_owners(outgoing)
+    requests = to_owners(jnp.pad(outgoing, ((0, 0), (0, 22), (0, 126))))[:, :2, :2]
     beside, wide = with_margins(first, second, from_above, from_below)
     windows = [to_owners(cut_windows(wide, requests, place)) for place in range(2)]
     ahead = (later[None, :] < later[:, None]) | (

time: 95.8 us -> 102 us (1.065); the launches traced: 94.4 us -> 102 us
  waiting for transfers between devices: 16.3 us -> 20.7 us
  starting transfers between devices: 27.7 us -> 30.7 us
    ppermute x4, waiting for transfers between devices: 0.01 us -> 3.07 us  [moved(): return lax.ppermute(values, axis, pairs)]
    all_to_all x3, starting transfers between devices: 16.5 us -> 19.3 us  [to_owners(): lax.all_to_all(values, 'strip', split_axis=0, concat_axis=0, tiled=True)]
    all_to_all x3, waiting for transfers between devices: 16.3 us -> 17.6 us  [to_owners(): lax.all_to_all(values, 'strip', split_axis=0, concat_axis=0, tiled=True)]
  transfers between devices with their start and end apart: 7 -> 7, of which waited for: 2 -> 3; matrix products, arithmetic and copies ran while one was open for 6% -> 5% of each run, Pallas kernels for 29% -> 27%
where the time goes in v2:
time: 102 us
  Pallas kernels  38.5 us (38%)
  starting transfers between devices  30.7 us (30%)
  waiting for transfers between devices  20.7 us (20%)
  other arithmetic  5.34 us (5%)
  local copies, waits for them, and re-layouts  3.82 us (4%)
  between operations  2.4 us (2%)
    pallas_call x2, Pallas kernels, surfaces_of(): pl.pallas_call(functools.partial(surface_kernel, phase=phase), out_shape=...  29.3 us
    all_to_all x3, starting transfers between devices, to_owners(): lax.all_to_all(values, 'strip', split_axis=0, concat_axis=0, tiled=True)  19.3 us
    all_to_all x3, waiting for transfers between devices, to_owners(): lax.all_to_all(values, 'strip', split_axis=0, concat_axis=0, tiled=True)  17.6 us
    ppermute x4, starting transfers between devices, moved(): return lax.ppermute(values, axis, pairs)  11.4 us
    pallas_call x2, Pallas kernels, cut_windows(): pl.pallas_call(functools.partial(cut_kernel, place=place), out_shape=jax....  9.22 us
    ppermute x4, waiting for transfers between devices, moved(): return lax.ppermute(values, axis, pairs)  3.07 us
  transfers between devices with their start and end apart: 7, of which 3 were waited for; matrix products, arithmetic and copies ran while one was open for 5% of the time, Pallas kernels for 27%

profile of v2, /device:TPU:1, one launch (start us, length us, event | category | flops | bytes accessed | tf_op | source)
XLA Modules:
  0.0 101.7 jit_solution(15223307615717273446)
XLA Ops:
  0.0 0.0 copy-start
  0.0 0.0 copy-start.1
  0.0 1.0 %fusion.19 = (bf16[64,512]{1,0:T(8,128)(2,1)S(1)}, bf16[64,512]{1,0:T(8,128)(2,1)S(1)}, bf16[64,512]{1,0:T(8,128)(2,1)S(1)}, bf16[64,512]{1,0:T(8,128)(2,1)S(1)}) fusion(bf16[512,512]{1,0:T(8,128)(2,1)} %first_ref.3, bf16[512,512]{1,0:T(8,128)(2,1)} %param.9), kind=kLoop, calls=%fused_computation.51 | loop fusion | bytes 524288 | tf_op jit(solution)/shard_map/slice | solution.py:364
  1.1 4.9 %collective-permute-start = (bf16[64,1024]{1,0:T(8,128)(2,1)S(1)}, bf16[64,1024]{1,0:T(8,128)(2,1)S(1)}, u32[]{:S(2)}, u32[]{:S(2)}) collective-permute-start(bf16[64,1024]{1,0:T(8,128)(2,1)S(1)} %pad_maximum_fusion.6), channel_id=1, source_target_pairs={{0,16},{16,32},{32,48},{48,64},{64,80},{80,96},{96,112},{1,17},{17... | collective-permute-start | bytes 393224 | tf_op jit(solution)/shard_map/ppermute | solution.py:360
  6.0 1.9 %collective-permute-start.1 = (bf16[64,1024]{1,0:T(8,128)(2,1)S(1)}, bf16[64,1024]{1,0:T(8,128)(2,1)S(1)}, u32[]{:S(2)}, u32[]{:S(2)}) collective-permute-start(bf16[64,1024]{1,0:T(8,128)(2,1)S(1)} %pad_maximum_fusion.7), channel_id=1, source_target_pairs={{16,0},{32,16},{48,32},{64,48},{80,64},{96,80},{112,96},{17,1},{33... | collective-permute-start | bytes 393224 | tf_op jit(solution)/shard_map/ppermute | solution.py:360
  8.0 1.5 %convert_reduce_fusion = (s32[]{:T(128)}, s32[16]{0:T(128)S(1)}) fusion(s32[16]{0:T(128)} %bitcast.33), kind=kLoop, calls=%fused_computation.25 | loop fusion | flops 1519 | bytes 132 | tf_op jit(solution)/shard_map/reduce_sum | solution.py:406
  9.5 0.7 multiply_add_fusion
  10.1 0.1 fusion.15
  10.2 0.8 add_add_fusion
  11.0 0.1 multiply_reduce_fusion
  11.1 0.1 copy.23
  11.2 0.7 pad.4
  11.9 6.8 %all-to-all-start = ((s32[16,24,128]{2,1,0:T(8,128)}), s32[16,24,128]{2,1,0:T(8,128)S(1)}, u32[]{:S(2)}, u32[]{:S(2)}) async-start(s32[16,24,128]{2,1,0:T(8,128)} %pad.4), calls=%async_computation | async-start | bytes 393216 | tf_op jit(solution)/shard_map/all_to_all | solution.py:381
  18.6 0.0 collective-permute-done
  18.7 0.0 copy-start.3
  18.7 0.0 collective-permute-done.1
  18.7 0.0 copy-start.5
  18.7 0.0 copy-done
  18.7 0.0 copy-done.1
  18.7 0.2 fusion.8
  18.9 3.3 %collective-permute-start.2 = (bf16[640,128]{1,0:T(8,128)(2,1)S(1)}, bf16[640,128]{1,0:T(8,128)(2,1)S(1)}, u32[]{:S(2)}, u32[]{:S(2)}) collective-permute-start(bf16[640,128]{1,0:T(8,128)(2,1)S(1)} %get-tuple-element.39), channel_id=1, source_target_pairs={{0,1},{1,2},{2,3},{3,4},{4,5},{5,6},{6,7},{7,8},{8,9},{9,10},{10,1... | collective-permute-start | bytes 491528 | tf_op jit(solution)/shard_map/ppermute | solution.py:360
  22.2 0.0 copy-done.3
  22.2 0.0 copy-done.5
  22.2 1.3 %collective-permute-start.3 = (bf16[640,128]{1,0:T(8,128)(2,1)S(1)}, bf16[640,128]{1,0:T(8,128)(2,1)S(1)}, u32[]{:S(2)}, u32[]{:S(2)}) collective-permute-start(bf16[640,128]{1,0:T(8,128)(2,1)S(1)} %get-tuple-element.40), channel_id=1, source_target_pairs={{1,0},{2,1},{3,2},{4,3},{5,4},{6,5},{7,6},{8,7},{9,8},{10,9},{11,1... | collective-permute-start | bytes 491528 | tf_op jit(solution)/shard_map/ppermute | solution.py:360
  23.5 2.3 %all-to-all-done = s32[16,24,128]{2,1,0:T(8,128)S(1)} async-done(((s32[16,24,128]{2,1,0:T(8,128)}), s32[16,24,128]{2,1,0:T(8,128)S(1)}, u32[]{:S(2)}, u32[]{:S(2)}) %all-to-all-start) | async-done | bytes 196640 | tf_op jit(solution)/shard_map/all_to_all | solution.py:381
  25.8 0.0 collective-permute-done.2
  25.8 0.1 fusion.21
  25.9 3.1 %collective-permute-done.3 = bf16[640,128]{1,0:T(8,128)(2,1)S(1)} collective-permute-done((bf16[640,128]{1,0:T(8,128)(2,1)S(1)}, bf16[640,128]{1,0:T(8,128)(2,1)S(1)}, u32[]{:S(2)}, u32[]{:S(2)}) %collective-permute-start.3) | collective-permute-done | bytes 163872 | tf_op jit(solution)/shard_map/ppermute | solution.py:360
  29.0 0.7 fusion.22
  29.7 0.4 pad_maximum_fusion.1.scene_ref
  30.2 4.6 %cut_windows.2 = bf16[16,288,128]{2,1,0:T(8,128)(2,1)} custom-call(s32[16,2,2]{2,1,0:T(2,128)S(1)} %slice.94.requests, bf16[640,640]{1,0:T(8,128)(2,1)S(1)} %pad_maximum_fusion.1.scene_ref), custom_call_target="tpu_custom_call" | custom-call | tf_op jit(solution)/shard_map/cut_windows/pallas_call | solution.py:61
  34.8 0.0 copy-start.8
  34.8 8.1 %all-to-all-start.1 = ((bf16[16,288,128]{2,1,0:T(8,128)(2,1)}), bf16[16,288,128]{2,1,0:T(8,128)(2,1)S(1)}, u32[]{:S(2)}, u32[]{:S(2)}) async-start(bf16[16,288,128]{2,1,0:T(8,128)(2,1)} %cut_windows.2), calls=%async_computation.1 | async-start | bytes 2359296 | tf_op jit(solution)/shard_map/all_to_all | solution.py:381
  42.9 0.0 copy-start.2
  42.9 0.0 copy-start.4
  42.9 0.0 copy-start.6
  43.7 0.2 convert_reduce_fusion.2
  43.9 0.2 select_reduce_fusion
  44.0 0.0 copy-done.8
  44.1 4.6 %cut_windows.3 = bf16[16,288,128]{2,1,0:T(8,128)(2,1)} custom-call(s32[16,2,2]{2,1,0:T(2,128)S(1)} %slice.94.requests, bf16[640,640]{1,0:T(8,128)(2,1)S(1)} %pad_maximum_fusion.1.scene_ref), custom_call_target="tpu_custom_call" | custom-call | tf_op jit(solution)/shard_map/cut_windows/pallas_call | solution.py:61
  48.7 0.0 copy-done.2
  48.7 0.0 copy-done.4
  48.7 0.0 copy-done.6
  48.7 0.4 pad_maximum_fusion.beside_ref
  49.1 0.0 copy-start.7
  49.1 15.3 %all-to-all-done.1.windows_ref = bf16[16,288,128]{2,1,0:T(8,128)(2,1)S(1)} async-done(((bf16[16,288,128]{2,1,0:T(8,128)(2,1)}), bf16[16,288,128]{2,1,0:T(8,128)(2,1)S(1)}, u32[]{:S(2)}, u32[]{:S(2)}) %all-to-all-start.1) | async-done | bytes 1179680 | tf_op jit(solution)/shard_map/all_to_all | solution.py:381
  64.5 4.4 %all-to-all-start.2 = ((bf16[16,288,128]{2,1,0:T(8,128)(2,1)}), bf16[16,288,128]{2,1,0:T(8,128)(2,1)}, u32[]{:S(2)}, u32[]{:S(2)}) async-start(bf16[16,288,128]{2,1,0:T(8,128)(2,1)} %cut_windows.3), calls=%async_computation.2 | async-start | bytes 2359296 | tf_op jit(solution)/shard_map/all_to_all | solution.py:381
  68.8 0.0 copy-done.7
  68.9 22.7 %surfaces_early.1 = (f32[17,24,256]{2,1,0:T(8,128)S(1)}, s32[1]{0:T(128)}) custom-call(s32[16]{0:T(128)S(1)} %bitcast.34, s32[16]{0:T(128)S(1)} %get-tuple-element.36.turns, s32[1]{0:T(128)} %sub.7.count_of, bf16[512,512]{1,0:T(8,128)(2,1)S(1)} %copy-done, bf16[640,640]{1,0:T(8,128)(2,1)S(1)} %pad_maximum_fusion.beside_ref, ...), custom_call_target="tpu_custom_call" | custom-call | flops 20000000000 | bytes 8000000 | tf_op jit(solution)/shard_map/surfaces_early/pallas_call | solution.py:329
  91.5 0.0 all-to-all-done.2.windows_ref
  91.5 6.6 %surfaces_later.1 = (f32[17,24,256]{2,1,0:T(8,128)S(1)}, s32[1]{0:T(128)}) custom-call(s32[16]{0:T(128)S(1)} %bitcast.35, s32[16]{0:T(128)S(1)} %get-tuple-element.35.turns, s32[1]{0:T(128)} %bitcast.1.count_of, bf16[512,512]{1,0:T(8,128)(2,1)S(1)} %copy-done, bf16[640,640]{1,0:T(8,128)(2,1)S(1)} %pad_maximum_fusion.beside_ref, ...), custom_call_target="tpu_custom_call" | custom-call | flops 20000000000 | bytes 8000000 | tf_op jit(solution)/shard_map/surfaces_later/pallas_call | solution.py:329
  99.5 0.2 conditional.1
  99.7 0.1 copy.20
  99.9 0.3 reshape.224
  100.2 0.1 slice_bitcast_fusion
  100.4 0.3 copy.22
  100.7 0.2 reshape.226
  100.9 0.8 broadcast_multiply_fusion
  (11 shorter events, 0.2 us)
Async XLA Ops:
  0.0 18.7 %copy-start = (bf16[512,512]{1,0:T(8,128)(2,1)S(1)}, bf16[512,512]{1,0:T(8,128)(2,1)}, u32[]{:S(2)}) copy-start(bf16[512,512]{1,0:T(8,128)(2,1)} %first_ref.3) | copy-start | bytes 1572868
  0.0 18.7 %copy-start.1 = (bf16[512,512]{1,0:T(8,128)(2,1)S(1)}, bf16[512,512]{1,0:T(8,128)(2,1)}, u32[]{:S(2)}) copy-start(bf16[512,512]{1,0:T(8,128)(2,1)} %param.9) | copy-start | bytes 1572868
  1.1 17.6 %collective-permute-start = (bf16[64,1024]{1,0:T(8,128)(2,1)S(1)}, bf16[64,1024]{1,0:T(8,128)(2,1)S(1)}, u32[]{:S(2)}, u32[]{:S(2)}) collective-permute-start(bf16[64,1024]{1,0:T(8,128)(2,1)S(1)} %pad_maximum_fusion.6), channel_id=1, source_target_pairs={{0,16},{16,32},{32,48},{48,64},{64,80},{80,96},{96,112},{1,17},{17... | collective-permute-start | bytes 393224 | tf_op jit(solution)/shard_map/ppermute | solution.py:360
  6.0 12.6 %collective-permute-start.1 = (bf16[64,1024]{1,0:T(8,128)(2,1)S(1)}, bf16[64,1024]{1,0:T(8,128)(2,1)S(1)}, u32[]{:S(2)}, u32[]{:S(2)}) collective-permute-start(bf16[64,1024]{1,0:T(8,128)(2,1)S(1)} %pad_maximum_fusion.7), channel_id=1, source_target_pairs={{16,0},{32,16},{48,32},{64,48},{80,64},{96,80},{112,96},{17,1},{33... | collective-permute-start | bytes 393224 | tf_op jit(solution)/shard_map/ppermute | solution.py:360
  11.9 14.0 %all-to-all-start = ((s32[16,24,128]{2,1,0:T(8,128)}), s32[16,24,128]{2,1,0:T(8,128)S(1)}, u32[]{:S(2)}, u32[]{:S(2)}) async-start(s32[16,24,128]{2,1,0:T(8,128)} %pad.4), calls=%async_computation | async-start | bytes 393216 | tf_op jit(solution)/shard_map/all_to_all | solution.py:381
  18.7 3.5 %copy-start.3 = (bf16[64,512]{1,0:T(8,128)(2,1)}, bf16[64,512]{1,0:T(8,128)(2,1)S(1)}, u32[]{:S(2)}) copy-start(bf16[64,512]{1,0:T(8,128)(2,1)S(1)} %get-tuple-element.49) | copy-start | bytes 196612
  18.7 3.5 %copy-start.5 = (bf16[64,512]{1,0:T(8,128)(2,1)}, bf16[64,512]{1,0:T(8,128)(2,1)S(1)}, u32[]{:S(2)}) copy-start(bf16[64,512]{1,0:T(8,128)(2,1)S(1)} %get-tuple-element.51) | copy-start | bytes 196612
  18.9 6.9 %collective-permute-start.2 = (bf16[640,128]{1,0:T(8,128)(2,1)S(1)}, bf16[640,128]{1,0:T(8,128)(2,1)S(1)}, u32[]{:S(2)}, u32[]{:S(2)}) collective-permute-start(bf16[640,128]{1,0:T(8,128)(2,1)S(1)} %get-tuple-element.39), channel_id=1, source_target_pairs={{0,1},{1,2},{2,3},{3,4},{4,5},{5,6},{6,7},{7,8},{8,9},{9,10},{10,1... | collective-permute-start | bytes 491528 | tf_op jit(solution)/shard_map/ppermute | solution.py:360
  22.2 6.8 %collective-permute-start.3 = (bf16[640,128]{1,0:T(8,128)(2,1)S(1)}, bf16[640,128]{1,0:T(8,128)(2,1)S(1)}, u32[]{:S(2)}, u32[]{:S(2)}) collective-permute-start(bf16[640,128]{1,0:T(8,128)(2,1)S(1)} %get-tuple-element.40), channel_id=1, source_target_pairs={{1,0},{2,1},{3,2},{4,3},{5,4},{6,5},{7,6},{8,7},{9,8},{10,9},{11,1... | collective-permute-start | bytes 491528 | tf_op jit(solution)/shard_map/ppermute | solution.py:360
  34.8 9.3 %copy-start.8 = (s32[1,1,16]{2,1,0:T(1,128)S(1)}, s32[1,1,16]{2,1,0:T(1,128)}, u32[]{:S(2)}) copy-start(s32[1,1,16]{2,1,0:T(1,128)} %param.13) | copy-start | bytes 196
  34.8 29.7 %all-to-all-start.1 = ((bf16[16,288,128]{2,1,0:T(8,128)(2,1)}), bf16[16,288,128]{2,1,0:T(8,128)(2,1)S(1)}, u32[]{:S(2)}, u32[]{:S(2)}) async-start(bf16[16,288,128]{2,1,0:T(8,128)(2,1)} %cut_windows.2), calls=%async_computation.1 | async-start | bytes 2359296 | tf_op jit(solution)/shard_map/all_to_all | solution.py:381
  42.9 5.8 %copy-start.2 = (bf16[640,64]{1,0:T(8,128)(2,1)S(1)}, bf16[640,64]{1,0:T(8,128)(2,1)}, u32[]{:S(2)}) copy-start(bf16[640,64]{1,0:T(8,128)(2,1)} %get-tuple-element.48) | copy-start | bytes 245764
  42.9 5.8 %copy-start.4 = (bf16[64,512]{1,0:T(8,128)(2,1)S(1)}, bf16[64,512]{1,0:T(8,128)(2,1)}, u32[]{:S(2)}) copy-start(bf16[64,512]{1,0:T(8,128)(2,1)} %copy-done.3) | copy-start | bytes 196612
  42.9 5.7 %copy-start.6 = (bf16[64,512]{1,0:T(8,128)(2,1)S(1)}, bf16[64,512]{1,0:T(8,128)(2,1)}, u32[]{:S(2)}) copy-start(bf16[64,512]{1,0:T(8,128)(2,1)} %copy-done.5) | copy-start | bytes 196612
  49.1 19.7 %copy-start.7 = (s32[1,1,16,1]{2,3,1,0:T(1,128)S(1)}, s32[1,1,16,1]{2,3,1,0:T(1,128)}, u32[]{:S(2)}) copy-start(s32[1,1,16,1]{2,3,1,0:T(1,128)} %param.10) | copy-start | bytes 196
  64.5 27.1 %all-to-all-start.2 = ((bf16[16,288,128]{2,1,0:T(8,128)(2,1)}), bf16[16,288,128]{2,1,0:T(8,128)(2,1)}, u32[]{:S(2)}, u32[]{:S(2)}) async-start(bf16[16,288,128]{2,1,0:T(8,128)(2,1)} %cut_windows.3), calls=%async_computation.2 | async-start | bytes 2359296 | tf_op jit(solution)/shard_map/all_to_all | solution.py:381

commit v3 on v1

--- a/solution.py
+++ b/solution.py
@@ -317,7 +317,18 @@
         build(jnp.minimum(2 * step + 2, 15), scratch[:6])
         return carry
 
-    lax.fori_loop(0, (count_of[0] + 1) // 2, pair, 0)
+    total = count_of[0]
+    lax.fori_loop(0, jnp.maximum(total - 1, 0) // 2, pair, 0)
+
+    @pl.when((total > 0) & (total % 2 == 0))
+    def _():
+        sums(total - 2, scratch[:6])
+        build(total - 1, scratch[6:])
+        sums(total - 1, scratch[6:])
+
+    @pl.when(total % 2 == 1)
+    def _():
+        sums(total - 1, scratch[:6])
 
 
 def surfaces_of(owners, turns, count_of, first, beside, windows, before=None):

time: 95.8 us -> 94.5 us (0.986)
  Pallas kernels: 38.5 us -> 37.4 us
    pallas_call x2, Pallas kernels: 29.3 us -> 28.2 us  [surfaces_of(): pl.pallas_call(functools.partial(surface_kernel, phase=phase), out_shape=...]
  transfers between devices with their start and end apart: 7 -> 7, of which waited for: 2 -> 2; matrix products, arithmetic and copies ran while one was open for 6% -> 7% of each run, Pallas kernels for 29% -> 29%
where the time goes in v3:
time: 94.5 us; the launch traced here: 93.1 us
  Pallas kernels  37.4 us (40%)
  starting transfers between devices  27.7 us (29%)
  waiting for transfers between devices  16.3 us (17%)
  other arithmetic  5.34 us (6%)
  local copies, waits for them, and re-layouts  3.91 us (4%)
  between operations  2.41 us (3%)
    pallas_call x2, Pallas kernels, surfaces_of(): pl.pallas_call(functools.partial(surface_kernel, phase=phase), out_shape=...  28.2 us
    all_to_all x3, starting transfers between devices, to_owners(): lax.all_to_all(values, 'strip', split_axis=0, concat_axis=0, tiled=True)  16.5 us
    all_to_all x3, waiting for transfers between devices, to_owners(): lax.all_to_all(values, 'strip', split_axis=0, concat_axis=0, tiled=True)  16.3 us
    ppermute x4, starting transfers between devices, moved(): return lax.ppermute(values, axis, pairs)  11.3 us
    pallas_call x2, Pallas kernels, cut_windows(): pl.pallas_call(functools.partial(cut_kernel, place=place), out_shape=jax....  9.21 us
  transfers between devices with their start and end apart: 7, of which 2 were waited for; matrix products, arithmetic and copies ran while one was open for 7% of the time, Pallas kernels for 29%

profile of v3, /device:TPU:1, one launch (start us, length us, event | category | flops | bytes accessed | tf_op | source)
XLA Modules:
  0.0 93.1 jit_solution(5080018204907503888)
XLA Ops:
  0.0 0.0 copy-start
  0.0 0.0 copy-start.1
  0.0 1.0 %fusion.19 = (bf16[64,512]{1,0:T(8,128)(2,1)S(1)}, bf16[64,512]{1,0:T(8,128)(2,1)S(1)}, bf16[64,512]{1,0:T(8,128)(2,1)S(1)}, bf16[64,512]{1,0:T(8,128)(2,1)S(1)}) fusion(bf16[512,512]{1,0:T(8,128)(2,1)} %first_ref.3, bf16[512,512]{1,0:T(8,128)(2,1)} %param.9), kind=kLoop, calls=%fused_computation.51 | loop fusion | bytes 524288 | tf_op jit(solution)/shard_map/slice | solution.py:376
  1.1 3.3 %collective-permute-start.1 = (bf16[64,1024]{1,0:T(8,128)(2,1)S(1)}, bf16[64,1024]{1,0:T(8,128)(2,1)S(1)}, u32[]{:S(2)}, u32[]{:S(2)}) collective-permute-start(bf16[64,1024]{1,0:T(8,128)(2,1)S(1)} %pad_maximum_fusion.7), channel_id=1, source_target_pairs={{16,0},{32,16},{48,32},{64,48},{80,64},{96,80},{112,96},{17,1},{33... | collective-permute-start | bytes 393224 | tf_op jit(solution)/shard_map/ppermute | solution.py:371
  4.4 3.5 %collective-permute-start = (bf16[64,1024]{1,0:T(8,128)(2,1)S(1)}, bf16[64,1024]{1,0:T(8,128)(2,1)S(1)}, u32[]{:S(2)}, u32[]{:S(2)}) collective-permute-start(bf16[64,1024]{1,0:T(8,128)(2,1)S(1)} %pad_maximum_fusion.6), channel_id=1, source_target_pairs={{0,16},{16,32},{32,48},{48,64},{64,80},{80,96},{96,112},{1,17},{17... | collective-permute-start | bytes 393224 | tf_op jit(solution)/shard_map/ppermute | solution.py:371
  8.0 1.5 %convert_reduce_fusion = (s32[]{:T(128)}, s32[16]{0:T(128)S(1)}) fusion(s32[16]{0:T(128)} %bitcast.33), kind=kLoop, calls=%fused_computation.25 | loop fusion | flops 1519 | bytes 132 | tf_op jit(solution)/shard_map/reduce_sum | solution.py:418
  9.5 0.7 multiply_add_fusion
  10.1 0.1 fusion.15
  10.2 0.8 add_add_fusion
  11.0 0.1 multiply_reduce_fusion
  11.1 0.1 reshape.223
  11.2 0.0 collective-permute-done.1
  11.2 0.0 collective-permute-done
  11.2 0.0 copy-start.3
  11.2 0.0 copy-start.5
  11.2 0.0 copy-done
  11.3 0.0 copy-done.1
  11.3 0.2 fusion.8
  11.4 3.1 %collective-permute-start.2 = (bf16[640,128]{1,0:T(8,128)(2,1)S(1)}, bf16[640,128]{1,0:T(8,128)(2,1)S(1)}, u32[]{:S(2)}, u32[]{:S(2)}) collective-permute-start(bf16[640,128]{1,0:T(8,128)(2,1)S(1)} %get-tuple-element.45), channel_id=1, source_target_pairs={{0,1},{1,2},{2,3},{3,4},{4,5},{5,6},{6,7},{7,8},{8,9},{9,10},{10,1... | collective-permute-start | bytes 491528 | tf_op jit(solution)/shard_map/ppermute | solution.py:371
  14.6 0.0 copy-done.3
  14.6 0.0 copy-done.5
  14.6 1.3 %collective-permute-start.3 = (bf16[640,128]{1,0:T(8,128)(2,1)S(1)}, bf16[640,128]{1,0:T(8,128)(2,1)S(1)}, u32[]{:S(2)}, u32[]{:S(2)}) collective-permute-start(bf16[640,128]{1,0:T(8,128)(2,1)S(1)} %get-tuple-element.46), channel_id=1, source_target_pairs={{1,0},{2,1},{3,2},{4,3},{5,4},{6,5},{7,6},{8,7},{9,8},{10,9},{11,1... | collective-permute-start | bytes 491528 | tf_op jit(solution)/shard_map/ppermute | solution.py:371
  15.9 0.8 copy.19
  16.7 7.6 %all-to-all-start = ((s32[16,2,2]{2,1,0:T(2,128)}), s32[16,2,2]{2,1,0:T(2,128)S(1)}, u32[]{:S(2)}, u32[]{:S(2)}) async-start(s32[16,2,2]{2,1,0:T(2,128)} %copy.19), calls=%async_computation | async-start | bytes 32768 | tf_op jit(solution)/shard_map/all_to_all | solution.py:392
  24.3 0.0 collective-permute-done.2
  24.3 0.1 fusion.21
  24.4 0.0 collective-permute-done.3
  24.4 0.7 fusion.22
  25.2 0.4 pad_maximum_fusion.1.scene_ref
  25.6 5.2 %all-to-all-done.requests = s32[16,2,2]{2,1,0:T(2,128)S(1)} async-done(((s32[16,2,2]{2,1,0:T(2,128)}), s32[16,2,2]{2,1,0:T(2,128)S(1)}, u32[]{:S(2)}, u32[]{:S(2)}) %all-to-all-start) | async-done | bytes 288 | tf_op jit(solution)/shard_map/all_to_all | solution.py:392
  30.8 4.6 %cut_windows.2 = bf16[16,288,128]{2,1,0:T(8,128)(2,1)} custom-call(s32[16,2,2]{2,1,0:T(2,128)S(1)} %all-to-all-done.requests, bf16[640,640]{1,0:T(8,128)(2,1)S(1)} %pad_maximum_fusion.1.scene_ref), custom_call_target="tpu_custom_call" | custom-call | tf_op jit(solution)/shard_map/cut_windows/pallas_call | solution.py:61
  35.4 0.0 copy-start.8
  35.4 3.8 %all-to-all-start.1 = ((bf16[16,288,128]{2,1,0:T(8,128)(2,1)}), bf16[16,288,128]{2,1,0:T(8,128)(2,1)S(1)}, u32[]{:S(2)}, u32[]{:S(2)}) async-start(bf16[16,288,128]{2,1,0:T(8,128)(2,1)} %cut_windows.2), calls=%async_computation.1 | async-start | bytes 2359296 | tf_op jit(solution)/shard_map/all_to_all | solution.py:392
  39.2 0.0 copy-start.2
  39.2 0.0 copy-start.4
  39.2 0.0 copy-start.6
  40.0 0.2 convert_reduce_fusion.2
  40.2 0.2 select_reduce_fusion
  40.3 0.0 copy-done.8
  40.4 4.6 %cut_windows.3 = bf16[16,288,128]{2,1,0:T(8,128)(2,1)} custom-call(s32[16,2,2]{2,1,0:T(2,128)S(1)} %all-to-all-done.requests, bf16[640,640]{1,0:T(8,128)(2,1)S(1)} %pad_maximum_fusion.1.scene_ref), custom_call_target="tpu_custom_call" | custom-call | tf_op jit(solution)/shard_map/cut_windows/pallas_call | solution.py:61
  45.0 0.0 copy-done.2
  45.0 0.0 copy-done.4
  45.0 0.0 copy-done.6
  45.0 0.4 pad_maximum_fusion.beside_ref
  45.4 0.0 copy-start.7
  45.4 11.1 %all-to-all-done.1.windows_ref = bf16[16,288,128]{2,1,0:T(8,128)(2,1)S(1)} async-done(((bf16[16,288,128]{2,1,0:T(8,128)(2,1)}), bf16[16,288,128]{2,1,0:T(8,128)(2,1)S(1)}, u32[]{:S(2)}, u32[]{:S(2)}) %all-to-all-start.1) | async-done | bytes 1179680 | tf_op jit(solution)/shard_map/all_to_all | solution.py:392
  56.6 5.0 %all-to-all-start.2 = ((bf16[16,288,128]{2,1,0:T(8,128)(2,1)}), bf16[16,288,128]{2,1,0:T(8,128)(2,1)}, u32[]{:S(2)}, u32[]{:S(2)}) async-start(bf16[16,288,128]{2,1,0:T(8,128)(2,1)} %cut_windows.3), calls=%async_computation.2 | async-start | bytes 2359296 | tf_op jit(solution)/shard_map/all_to_all | solution.py:392
  61.6 0.0 copy-done.7
  61.6 22.0 %surfaces_early.1 = (f32[17,24,256]{2,1,0:T(8,128)S(1)}, s32[1]{0:T(128)}) custom-call(s32[16]{0:T(128)S(1)} %bitcast.34, s32[16]{0:T(128)S(1)} %get-tuple-element.42.turns, s32[1]{0:T(128)} %sub.7.count_of, bf16[512,512]{1,0:T(8,128)(2,1)S(1)} %copy-done, bf16[640,640]{1,0:T(8,128)(2,1)S(1)} %pad_maximum_fusion.beside_ref, ...), custom_call_target="tpu_custom_call" | custom-call | flops 20000000000 | bytes 8000000 | tf_op jit(solution)/shard_map/surfaces_early/pallas_call | solution.py:340
  83.6 0.0 all-to-all-done.2.windows_ref
  83.6 6.2 %surfaces_later.1 = (f32[17,24,256]{2,1,0:T(8,128)S(1)}, s32[1]{0:T(128)}) custom-call(s32[16]{0:T(128)S(1)} %bitcast.35, s32[16]{0:T(128)S(1)} %get-tuple-element.41.turns, s32[1]{0:T(128)} %bitcast.1.count_of, bf16[512,512]{1,0:T(8,128)(2,1)S(1)} %copy-done, bf16[640,640]{1,0:T(8,128)(2,1)S(1)} %pad_maximum_fusion.beside_ref, ...), custom_call_target="tpu_custom_call" | custom-call | flops 20000000000 | bytes 8000000 | tf_op jit(solution)/shard_map/surfaces_later/pallas_call | solution.py:340
  91.2 0.1 copy.20
  91.3 0.3 reshape.224
  91.6 0.1 slice_bitcast_fusion
  91.9 0.3 copy.22
  92.1 0.2 reshape.226
  92.3 0.8 broadcast_multiply_fusion
  (11 shorter events, 0.2 us)
Async XLA Ops:
  0.0 11.2 %copy-start = (bf16[512,512]{1,0:T(8,128)(2,1)S(1)}, bf16[512,512]{1,0:T(8,128)(2,1)}, u32[]{:S(2)}) copy-start(bf16[512,512]{1,0:T(8,128)(2,1)} %first_ref.3) | copy-start | bytes 1572868
  0.0 11.3 %copy-start.1 = (bf16[512,512]{1,0:T(8,128)(2,1)S(1)}, bf16[512,512]{1,0:T(8,128)(2,1)}, u32[]{:S(2)}) copy-start(bf16[512,512]{1,0:T(8,128)(2,1)} %param.9) | copy-start | bytes 1572868
  1.1 10.1 %collective-permute-start.1 = (bf16[64,1024]{1,0:T(8,128)(2,1)S(1)}, bf16[64,1024]{1,0:T(8,128)(2,1)S(1)}, u32[]{:S(2)}, u32[]{:S(2)}) collective-permute-start(bf16[64,1024]{1,0:T(8,128)(2,1)S(1)} %pad_maximum_fusion.7), channel_id=1, source_target_pairs={{16,0},{32,16},{48,32},{64,48},{80,64},{96,80},{112,96},{17,1},{33... | collective-permute-start | bytes 393224 | tf_op jit(solution)/shard_map/ppermute | solution.py:371
  4.4 6.8 %collective-permute-start = (bf16[64,1024]{1,0:T(8,128)(2,1)S(1)}, bf16[64,1024]{1,0:T(8,128)(2,1)S(1)}, u32[]{:S(2)}, u32[]{:S(2)}) collective-permute-start(bf16[64,1024]{1,0:T(8,128)(2,1)S(1)} %pad_maximum_fusion.6), channel_id=1, source_target_pairs={{0,16},{16,32},{32,48},{48,64},{64,80},{80,96},{96,112},{1,17},{17... | collective-permute-start | bytes 393224 | tf_op jit(solution)/shard_map/ppermute | solution.py:371
  11.2 3.4 %copy-start.3 = (bf16[64,512]{1,0:T(8,128)(2,1)}, bf16[64,512]{1,0:T(8,128)(2,1)S(1)}, u32[]{:S(2)}) copy-start(bf16[64,512]{1,0:T(8,128)(2,1)S(1)} %get-tuple-element.55) | copy-start | bytes 196612
  11.2 3.3 %copy-start.5 = (bf16[64,512]{1,0:T(8,128)(2,1)}, bf16[64,512]{1,0:T(8,128)(2,1)S(1)}, u32[]{:S(2)}) copy-start(bf16[64,512]{1,0:T(8,128)(2,1)S(1)} %get-tuple-element.57) | copy-start | bytes 196612
  11.4 12.9 %collective-permute-start.2 = (bf16[640,128]{1,0:T(8,128)(2,1)S(1)}, bf16[640,128]{1,0:T(8,128)(2,1)S(1)}, u32[]{:S(2)}, u32[]{:S(2)}) collective-permute-start(bf16[640,128]{1,0:T(8,128)(2,1)S(1)} %get-tuple-element.45), channel_id=1, source_target_pairs={{0,1},{1,2},{2,3},{3,4},{4,5},{5,6},{6,7},{7,8},{8,9},{9,10},{10,1... | collective-permute-start | bytes 491528 | tf_op jit(solution)/shard_map/ppermute | solution.py:371
  14.6 9.9 %collective-permute-start.3 = (bf16[640,128]{1,0:T(8,128)(2,1)S(1)}, bf16[640,128]{1,0:T(8,128)(2,1)S(1)}, u32[]{:S(2)}, u32[]{:S(2)}) collective-permute-start(bf16[640,128]{1,0:T(8,128)(2,1)S(1)} %get-tuple-element.46), channel_id=1, source_target_pairs={{1,0},{2,1},{3,2},{4,3},{5,4},{6,5},{7,6},{8,7},{9,8},{10,9},{11,1... | collective-permute-start | bytes 491528 | tf_op jit(solution)/shard_map/ppermute | solution.py:371
  16.7 14.1 %all-to-all-start = ((s32[16,2,2]{2,1,0:T(2,128)}), s32[16,2,2]{2,1,0:T(2,128)S(1)}, u32[]{:S(2)}, u32[]{:S(2)}) async-start(s32[16,2,2]{2,1,0:T(2,128)} %copy.19), calls=%async_computation | async-start | bytes 32768 | tf_op jit(solution)/shard_map/all_to_all | solution.py:392
  35.4 5.0 %copy-start.8 = (s32[1,1,16]{2,1,0:T(1,128)S(1)}, s32[1,1,16]{2,1,0:T(1,128)}, u32[]{:S(2)}) copy-start(s32[1,1,16]{2,1,0:T(1,128)} %param.13) | copy-start | bytes 196
  35.4 21.2 %all-to-all-start.1 = ((bf16[16,288,128]{2,1,0:T(8,128)(2,1)}), bf16[16,288,128]{2,1,0:T(8,128)(2,1)S(1)}, u32[]{:S(2)}, u32[]{:S(2)}) async-start(bf16[16,288,128]{2,1,0:T(8,128)(2,1)} %cut_windows.2), calls=%async_computation.1 | async-start | bytes 2359296 | tf_op jit(solution)/shard_map/all_to_all | solution.py:392
  39.2 5.8 %copy-start.2 = (bf16[640,64]{1,0:T(8,128)(2,1)S(1)}, bf16[640,64]{1,0:T(8,128)(2,1)}, u32[]{:S(2)}) copy-start(bf16[640,64]{1,0:T(8,128)(2,1)} %get-tuple-element.54) | copy-start | bytes 245764
  39.2 5.8 %copy-start.4 = (bf16[64,512]{1,0:T(8,128)(2,1)S(1)}, bf16[64,512]{1,0:T(8,128)(2,1)}, u32[]{:S(2)}) copy-start(bf16[64,512]{1,0:T(8,128)(2,1)} %copy-done.3) | copy-start | bytes 196612
  39.2 5.7 %copy-start.6 = (bf16[64,512]{1,0:T(8,128)(2,1)S(1)}, bf16[64,512]{1,0:T(8,128)(2,1)}, u32[]{:S(2)}) copy-start(bf16[64,512]{1,0:T(8,128)(2,1)} %copy-done.5) | copy-start | bytes 196612
  45.4 16.2 %copy-start.7 = (s32[1,1,16,1]{2,3,1,0:T(1,128)S(1)}, s32[1,1,16,1]{2,3,1,0:T(1,128)}, u32[]{:S(2)}) copy-start(s32[1,1,16,1]{2,3,1,0:T(1,128)} %param.10) | copy-start | bytes 196
  56.6 27.0 %all-to-all-start.2 = ((bf16[16,288,128]{2,1,0:T(8,128)(2,1)}), bf16[16,288,128]{2,1,0:T(8,128)(2,1)}, u32[]{:S(2)}, u32[]{:S(2)}) async-start(bf16[16,288,128]{2,1,0:T(8,128)(2,1)} %cut_windows.3), calls=%async_computation.2 | async-start | bytes 2359296 | tf_op jit(solution)/shard_map/all_to_all | solution.py:392
